TPU v7x, 32 devices: a whole 2x2x4 slice. The times are simulated.
32 devices in a mesh: pb: 8 (over z, x), ka: 4 (over y, core).
Axes of the slice: x: 2, y: 2, z: 4, core: 2. Of those that a mesh axis runs over, the one named last changes fastest.
Arguments:
- valence: float32 [208, 64, 1024], P('pb', 'ka'), may hold values from -6 to 6
- conduction: bfloat16 [208, 196, 1024], P('pb', None, 'ka'), may hold values from -0.0024414062 to 0.0024414062
- screened: float32 [8, 1024, 1024], P('pb'), may hold values from -1 to 3, as said below
- momentum: int32 [208, 1], P('pb'), may hold values from 0 to 7; in each aligned block of 26 rows (0 to 25, 26 to 51, ...) at most 6 rows name the same one
- kpairs: int32 [208, 2], P('pb'), may hold values from 0 to 7
- kpoint_slot: int32 [8], replicated, may hold values from 0 to 7, each once
- trial_blocks: float32 [8, 14336], P('pb', 'ka'), may hold values from -6 to 6
Outputs:
- response: float32 [8, 14336], P('pb', 'ka')
Inputs may be any that keep to these rules, and one draw needn't show every extreme that they name: Among the k-pairs of one index of pb (rows i * 26 to (i + 1) * 26 - 1), at most 6 share a momentum transfer. `kpoint_slot`: each row number appears once. `screened`: each matrix is symmetric.
All inputs are finite; a program needn't handle non-finite values.
Results may differ from a plain program's by a relative error of at most 0.0003.
Values sent between devices are 32-bit elements; how exact they have to be, the bound alone decides.
A program may use at most 128 MiB of HBM per device.

v0:
```python
import jax
import jax.numpy as jnp
from jax import lax
from jax.sharding import PartitionSpec as P

VB = 8
CB = 14


def local(valence, conduction, screened, momentum, kpairs, kpoint_slot, trial_blocks):
    highest = lax.Precision.HIGHEST
    pair_dev = valence.shape[0]
    owners = lax.axis_size("pb")
    capacity = max(2, 2 * pair_dev // owners)
    slot_count = owners * capacity
    target = momentum[:, 0]
    indices = jnp.arange(pair_dev, dtype=jnp.int32)
    earlier = (target[:, None] == target[None, :]) & (indices[None, :] < indices[:, None])
    position = target * capacity + jnp.sum(earlier.astype(jnp.int32), axis=1)
    matches = position[None, :] == jnp.arange(slot_count, dtype=jnp.int32)[:, None]
    source = jnp.sum(jnp.where(matches, indices[None, :], 0), axis=1)
    filled = jnp.any(matches, axis=1)
    outgoing = jnp.where(filled[:, None, None], jnp.take(valence, source, axis=0), 0.0)
    outgoing = outgoing.reshape(owners, capacity, valence.shape[1], valence.shape[2])
    matrix = screened[0]
    product = jnp.einsum(
        "scrg,gh->scrh",
        lax.all_to_all(outgoing, "pb", split_axis=0, concat_axis=0, tiled=True),
        matrix,
        precision=highest,
        preferred_element_type=jnp.float32,
    )
    returned = lax.all_to_all(product, "pb", split_axis=0, concat_axis=0, tiled=True)
    by_slot = returned.reshape(slot_count, returned.shape[2], returned.shape[3])
    rows_back = jnp.take(by_slot, position, axis=0)
    columns = lax.all_to_all(rows_back, "ka", split_axis=2, concat_axis=1, tiled=True)
    conduct_wide = conduction.astype(jnp.float32)
    partial_kernel = jnp.einsum(
        "prg,pbg->prb", columns, conduct_wide, precision=highest, preferred_element_type=jnp.float32
    )
    kernel = lax.psum(partial_kernel, "ka")
    gathered = lax.all_gather(trial_blocks, "pb", axis=0, tiled=True)
    kpoint_count = gathered.shape[0]
    local_trials = gathered.shape[1] // (VB * CB)
    blocks = gathered.reshape(kpoint_count, local_trials, VB, CB)
    slot_near = jnp.take(kpoint_slot, kpairs[:, 0])
    slot_far = jnp.take(kpoint_slot, kpairs[:, 1])
    near_trials = jnp.take(blocks, slot_near, axis=0)
    far_trials = jnp.take(blocks, slot_far, axis=0)
    kernel_blocks = kernel.reshape(pair_dev, VB, VB, CB, CB)
    direct = jnp.einsum("pvwcd,pnwd->pnvc", kernel_blocks, far_trials, precision=highest)
    mirror = jnp.einsum("pvwcd,pnvc->pnwd", kernel_blocks, near_trials, precision=highest)
    kpoint_rows = jnp.arange(kpoint_count, dtype=jnp.int32)[:, None]
    onehot_near = (slot_near[None, :] == kpoint_rows).astype(jnp.float32)
    onehot_far = (slot_far[None, :] == kpoint_rows).astype(jnp.float32)
    summed = jnp.dot(
        onehot_near,
        direct.reshape(pair_dev, -1),
        precision=highest,
        preferred_element_type=jnp.float32,
    )
    summed = summed + jnp.dot(
        onehot_far,
        mirror.reshape(pair_dev, -1),
        precision=highest,
        preferred_element_type=jnp.float32,
    )
    return lax.psum_scatter(summed, "pb", scatter_dimension=0, tiled=True)


def solution(mesh):
    return jax.shard_map(
        local,
        mesh=mesh,
        in_specs=(
            P("pb", "ka", None),
            P("pb", None, "ka"),
            P("pb", None, None),
            P("pb", None),
            P("pb", None),
            P(),
            P("pb", "ka"),
        ),
        out_specs=P("pb", "ka"),
        check_vma=False,
    )
```

profile of v0, /device:TPU:0, one launch (start us, length us, event | category | flops | bytes accessed | tf_op | source)
XLA Modules:
  0.0 669.2 jit_solution(16367301800515947824)
XLA Ops:
  6.5 1.0 convert_reduce_fusion
  8.6 3.9 gather_fusion
  12.4 2.3 select_select_fusion
  14.7 78.0 %all_to_all.28 = f32[8,6,16,1024]{3,2,1,0:T(8,128)S(1)} all-to-all(f32[8,6,16,1024]{3,2,1,0:T(8,128)S(1)} %select_select_fusion), channel_id=1, replica_groups=mesh['pb'=8,'ka'=4] {'pb'}, dimensions={0} | all-to-all | bytes 6291456 | tf_op jit(solution)/shard_map/all_to_all | solution.py:28
  92.8 11.8 %fusion = f32[8,6,16,1024]{3,2,1,0:T(8,128)} fusion(f32[8,6,16,1024]{3,2,1,0:T(8,128)S(1)} %all_to_all.28, f32[1,1024,1024]{2,1,0:T(8,128)S(1)} %copy-done.3), kind=kOutput, calls=%fused_computation.7 | convolution fusion | flops 9663676416 | bytes 10485760 | tf_op jit(solution)/shard_map/scrg,gh->scrh/dot_general | solution.py:26
  104.6 5.0 all-to-all-start.1
  109.7 69.8 %all-to-all-done.1 = f32[8,6,16,1024]{3,2,1,0:T(8,128)} async-done(((f32[8,6,16,1024]{3,2,1,0:T(8,128)}), f32[8,6,16,1024]{3,2,1,0:T(8,128)}, u32[]{:S(2)}, u32[]{:S(2)}) %all-to-all-start.1) | async-done | bytes 3145760 | tf_op jit(solution)/shard_map/all_to_all | solution.py:33
  179.5 3.8 gather_fusion.1
  183.3 2.9 broadcast_select_fusion
  186.2 7.5 %copy.47 = f32[26,16,1024]{0,1,2:T(8,128)} copy(f32[26,16,1024]{2,1,0:T(8,128)} %broadcast_select_fusion) | data formatting | bytes 3407872 | tf_op jit(solution)/shard_map/jit(_take)/select_n | solution.py:35
  193.6 11.2 %reshape.142 = f32[4,1,106496]{2,1,0:T(1,128)} reshape(f32[1024,16,26]{2,1,0:T(8,128)} %bitcast.69) | data formatting | bytes 3407872
  204.9 4.5 all-to-all-start.2
  210.9 30.6 %all-gather = f32[8,1,3584]{2,1,0:T(1,128)S(1)} all-gather(f32[1,1,3584]{2,1,0:T(1,128)S(1)} %bitcast.74), channel_id=1, replica_groups=mesh['pb'=8,'ka'=4] {'pb'}, dimensions={0}, use_global_device_ids=true | all-gather | bytes 129024 | tf_op jit(solution)/shard_map/all_gather | solution.py:42
  241.7 2.1 reshape.67
  243.8 1.7 copy.46
  246.0 7.8 %reduce.1 = f32[4,106496]{1,0:T(4,128)} reduce(f32[4,1,106496]{2,1,0:T(1,128)} %all-to-all-done.2, f32[]{:T(128)} %broadcast.182), dimensions={1}, to_apply=%all_to_all.21.reduce_sub_computation | reduce | bytes 3407876 | tf_op jit(solution)/shard_map/all_to_all | solution.py:36
  253.8 15.0 %reshape.143 = f32[1024,16,26]{2,1,0:T(8,128)} reshape(f32[4,106496]{1,0:T(4,128)} %reduce.1) | data formatting | bytes 3407872
  268.9 7.8 %copy.48 = f32[26,16,4,256]{3,1,2,0:T(8,128)} copy(f32[26,16,4,256]{0,1,3,2:T(8,128)} %bitcast.70) | data formatting | bytes 3407872 | tf_op jit(solution)/shard_map/all_to_all | solution.py:36
  276.7 5.3 fusion.18
  282.0 5.8 copy.49
  287.8 14.5 %copy.50 = f32[26,8,8,14,14]{3,2,4,1,0:T(8,128)} copy(f32[26,8,8,14,14]{0,2,1,4,3:T(8,128)} %bitcast.71) | data formatting | bytes 2609152 | tf_op jit(solution)/shard_map/reshape | solution.py:50
  302.4 1.8 gather_fusion.4
  304.9 207.2 %all-reduce.4.cloned.1.call-done = f32[26,8,8,14,14]{3,2,4,1,0:T(8,128)} async-done(((f32[26,8,8,14,14]{3,2,4,1,0:T(8,128)}), f32[26,8,8,14,14]{3,2,4,1,0:T(8,128)}) %all-reduce.4.cloned.1.call-update) | async-done | bytes 1304592 | tf_op jit(solution)/shard_map/psum | solution.py:41
  512.0 22.7 %convolution_bitcast_fusion.1 = f32[26,32,8,14]{1,3,2,0:T(8,128)} fusion(f32[26,8,8,14,14]{3,2,4,1,0:T(8,128)} %all-reduce.4.cloned.1.call-done, f32[26,32,8,14]{1,2,3,0:T(8,128)} %gather_fusion.4, pred[26]{0:T(512)(128)(4,1)S(1)} %get-tuple-element.13), kind=kOutput, calls=%fused_computation.11 | convolution fusion | flops 125332480 | bytes 2050074 | tf_op jit(solution)/shard_map/pvwcd,pnwd->pnvc/dot_general | solution.py:51
  534.8 3.7 copy.51
  538.5 4.0 reshape.70
  542.7 16.4 %copy.53 = f32[26,8,8,14,14]{4,1,3,2,0:T(8,128)} copy(f32[26,8,8,14,14]{3,2,4,1,0:T(8,128)} %all-reduce.4.cloned.1.call-done) | data formatting | bytes 2609152 | tf_op jit(solution)/shard_map/psum | solution.py:41
  559.1 22.7 %convolution_bitcast_fusion = f32[26,32,8,14]{1,3,2,0:T(8,128)} fusion(f32[26,8,8,14,14]{4,1,3,2,0:T(8,128)} %copy.53, f32[26,32,8,14]{1,2,3,0:T(8,128)S(1)} %gather_fusion.5, pred[26]{0:T(512)(128)(4,1)S(1)} %get-tuple-element.6), kind=kOutput, calls=%fused_computation.10 | convolution fusion | flops 125332480 | bytes 2050074 | tf_op jit(solution)/shard_map/pvwcd,pnvc->pnwd/dot_general | solution.py:52
  581.8 3.8 copy.54
  585.6 4.0 reshape.71
  591.2 68.8 %all-reduce.6.cloned.1.call-done = f32[8,3584]{1,0:T(8,128)} async-done(((f32[8,3584]{1,0:T(8,128)}), f32[8,3584]{1,0:T(8,128)}) %all-reduce.6.cloned.1.call-update) | async-done | bytes 114704
  660.0 2.1 constant_dynamic-slice_fusion
  (46 shorter events, 5.9 us)
Async XLA Ops:
  6.5 270.2 %copy-start = (bf16[26,196,256]{2,1,0:T(8,128)(2,1)S(1)}, bf16[26,196,256]{2,1,0:T(8,128)(2,1)}, u32[]{:S(2)}) copy-start(bf16[26,196,256]{2,1,0:T(8,128)(2,1)} %param.12) | copy-start | bytes 7827460
  14.7 78.0 %copy-start.3 = (f32[1,1024,1024]{2,1,0:T(8,128)S(1)}, f32[1,1024,1024]{2,1,0:T(8,128)}, u32[]{:S(2)}) copy-start(f32[1,1024,1024]{2,1,0:T(8,128)} %param.13) | copy-start | bytes 12582916
  104.6 5.0 copy-start.6
  104.6 74.9 %all-to-all-start.1 = ((f32[8,6,16,1024]{3,2,1,0:T(8,128)}), f32[8,6,16,1024]{3,2,1,0:T(8,128)}, u32[]{:S(2)}, u32[]{:S(2)}) async-start(f32[8,6,16,1024]{3,2,1,0:T(8,128)} %fusion), calls=%async_computation.1 | async-start | bytes 6291456 | tf_op jit(solution)/shard_map/all_to_all | solution.py:33
  204.8 4.6 copy-start.5
  204.8 4.6 copy-start.2
  204.8 6.0 copy-start.4
  204.9 40.7 %all-to-all-start.2 = ((f32[4,1,106496]{2,1,0:T(1,128)}), f32[4,1,106496]{2,1,0:T(1,128)}, u32[]{:S(2)}, u32[]{:S(2)}) async-start(f32[4,1,106496]{2,1,0:T(1,128)} %reshape.142), calls=%async_computation.2 | async-start | bytes 3407872 | tf_op jit(solution)/shard_map/all_to_all | solution.py:36
  209.4 302.7 %all-reduce.4.cloned.1.call-start = ((), (), s32[]{:S(2)}) async-start(), calls=%async_computation.3 | async-start | bytes 23855104 | tf_op jit(solution)/shard_map/psum | solution.py:41
  302.3 357.7 %all-reduce.6.cloned.1.call-start = ((), (), s32[]{:S(2)}) async-start(), calls=%async_computation.4 | async-start | bytes 229376
  581.8 80.4 %copy-start.1 = (bf16[26,196,256]{2,1,0:T(8,128)(2,1)S(1)}, bf16[26,196,256]{2,1,0:T(8,128)(2,1)}, u32[]{:S(2)}) copy-start(bf16[26,196,256]{2,1,0:T(8,128)(2,1)} %param.12) | copy-start | bytes 7827460
  585.6 5.0 copy-start.7
Sparse Core Ops, SparseCore 0:
  302.4 209.5 all-reduce.3
  590.7 69.3 all-reduce.5
where the time goes:
time: 677 us; the launch traced here: 669 us
  waiting for transfers between devices  346 us (51%)
  local copies, waits for them, and re-layouts  112 us (17%)
  blocking collectives  109 us (16%)
  matrix products  63.7 us (9%)
  other arithmetic  15.2 us (2%)
  between operations  13.8 us (2%)
  starting transfers between devices  9.63 us (1%)
    psum x1, waiting for transfers between devices, local(): kernel = lax.psum(partial_kernel, 'ka')  207 us
    all_to_all x1, blocking collectives, local(): lax.all_to_all(outgoing, 'pb', split_axis=0, concat_axis=0, tiled=True)  78 us
    all_to_all x1, waiting for transfers between devices, local(): lax.all_to_all(product, 'pb', split_axis=0, concat_axis=0, tiled=True)  69.8 us
    unnamed x3, waiting for transfers between devices  68.9 us
    all_gather x1, blocking collectives, local(): gathered = lax.all_gather(trial_blocks, 'pb', axis=0, tiled=True)  30.6 us
    unnamed x20, local copies, waits for them, and re-layouts  29.1 us
    dot_general x1, matrix products, local(): jnp.einsum('pvwcd,pnwd->pnvc', kernel_blocks, far_trials, precision=highest)  22.7 us
    dot_general x1, matrix products, local(): jnp.einsum('pvwcd,pnvc->pnwd', kernel_blocks, near_trials, precision=high...  22.7 us
  transfers between devices with their start and end apart: 4, of which 3 were waited for; matrix products, arithmetic and copies ran while one was open for 1% of the time, Pallas kernels for 0%

commit v1 on v0

--- a/solution.py
+++ b/solution.py
@@ -1,13 +1,304 @@
+import functools
+
 import jax
 import jax.numpy as jnp
 from jax import lax
+from jax.experimental import pallas as pl
+from jax.experimental.pallas import tpu as pltpu
 from jax.sharding import PartitionSpec as P
 
 VB = 8
 CB = 14
+MESH = pl.DeviceIdType.MESH
+NT = (((1,), (1,)), ((), ()))
+
+
+def dot_nt(a, b):
+    return lax.dot_general(a, b, NT, preferred_element_type=jnp.float32)
+
+
+def halves(x):
+    high = x.astype(jnp.bfloat16)
+    return high, (x - high.astype(jnp.float32)).astype(jnp.bfloat16)
+
+
+def ring_index(place, n):
+    return jnp.where(place < n // 2, 2 * place, 2 * (n - 1 - place) + 1)
+
+
+def kernel_blocks_kernel(
+    n, parts, capacity,
+    source_ref, v_ref, c_ref, w_ref, x_ref,
+    k_ref, xout_ref,
+    w_all, v_all, v_high, v_low, g_high, g_low, k_part, k_in, x_all,
+    local_sems, v_send, v_recv, ring_send, ring_recv, k_send, k_recv, x_send, x_recv, xk_send, xk_recv,
+):
+    pb, ka = lax.axis_index("pb"), lax.axis_index("ka")
+    place = jnp.where(pb % 2 == 0, pb // 2, n - 1 - pb // 2)
+    right = ring_index((place + 1) % n, n)
+    left = ring_index((place + n - 1) % n, n)
+    partner = ka + 1 - 2 * (ka % 2)
+    across = (ka + 2) % parts
+    rows = v_ref.shape[1]
+    depth = w_all.shape[1]
+    pairs = v_ref.shape[0]
+
+    own_w = pltpu.make_async_copy(w_ref.at[0, pl.ds(pl.multiple_of(ka * depth, depth), depth), :], w_all.at[place], local_sems.at[0])
+    own_v = pltpu.make_async_copy(v_ref, v_all.at[ka], local_sems.at[1])
+    own_w.start()
+    own_v.start()
+    x_all[ka, pb] = x_ref[...]
+
+    barrier = pltpu.get_barrier_semaphore()
+    for d in range(1, n):
+        pl.semaphore_signal(barrier, inc=1, device_id=((pb + d) % n, ka), device_id_type=MESH)
+    for d in range(1, parts):
+        pl.semaphore_signal(barrier, inc=1, device_id=(pb, (ka + d) % parts), device_id_type=MESH)
+    pl.semaphore_wait(barrier, n + parts - 2)
+
+    def remote(src, dst, send, recv, to):
+        return pltpu.make_async_remote_copy(src_ref=src, dst_ref=dst, send_sem=send, recv_sem=recv, device_id=to, device_id_type=MESH)
+
+    def ring(step):
+        ahead = (place + n - step) % n
+        behind = (place + step) % n
+        if step < n // 2 - 1:
+            go, back = w_all.at[ahead], w_all.at[behind]
+        else:
+            go = w_all.at[ahead, pl.ds(0, depth // 2)]
+            back = w_all.at[behind, pl.ds(depth // 2, depth // 2)]
+        return (
+            remote(go, go, ring_send.at[step, 0], ring_recv.at[step, 0], (right, ka)),
+            remote(back, back, ring_send.at[step, 1], ring_recv.at[step, 1], (left, ka)),
+        )
+
+    own_v.wait()
+    v_across = remote(v_all.at[ka], v_all.at[ka], v_send.at[1], v_recv.at[1], (pb, across))
+    v_partner = remote(v_all.at[ka], v_all.at[ka], v_send.at[0], v_recv.at[0], (pb, partner))
+    v_pass = remote(v_all.at[across], v_all.at[across], v_send.at[2], v_recv.at[2], (pb, partner))
+    own_w.wait()
+    copies = ring(0)
+    copies[0].start()
+    copies[1].start()
+    v_across.start()
+    v_partner.start()
+    x_copies = [
+        remote(x_all.at[ka, pb], x_all.at[ka, pb], x_send.at[d - 1], x_recv.at[d - 1], ((pb + d) % n, ka)) for d in range(1, n)
+    ]
+    for copy in x_copies:
+        copy.start()
+
+    def k_copy(q, d):
+        to = (ka + d) % parts
+        return remote(
+            k_part.at[q, :, pl.ds(pl.multiple_of(to * rows, rows), rows), :],
+            k_in.at[d - 1, q],
+            k_send.at[q, d - 1], k_recv.at[q, d - 1], (pb, to),
+        )
+
+    def block(k, carry):
+        at = (place + n + ((k + 1) // 2) * (2 * (k % 2) - 1)) % n
+        q = ring_index(at, n)
+        high, low = halves(w_all[at])
+        for s in range(capacity):
+            p = source_ref[q * capacity + s]
+            g_high[pl.ds(s * parts * rows, parts * rows), :] = v_high[p]
+            g_low[pl.ds(s * parts * rows, parts * rows), :] = v_low[p]
+        screened = dot_nt(g_high[...], high) + (dot_nt(g_high[...], low) + dot_nt(g_low[...], high))
+        s_high, s_low = halves(screened)
+        for s in range(capacity):
+            span = slice(s * parts * rows, (s + 1) * parts * rows)
+            conduct = c_ref[source_ref[q * capacity + s]]
+            k_part[q, s] = dot_nt(s_high[span], conduct) + dot_nt(s_low[span], conduct)
+        for d in range(1, parts):
+            k_copy(q, d).start()
+        return carry
+
+    for step in range(1, n // 2):
+        later = ring(step)
+        copies[0].wait_recv()
+        later[0].start()
+        copies[1].wait_recv()
+        later[1].start()
+        copies[0].wait_send()
+        copies[1].wait_send()
+        copies = later
+        if step == 1:
+            for copy in x_copies:
+                copy.wait()
+            xk_copies = [
+                remote(x_all.at[ka], x_all.at[ka], xk_send.at[d - 1], xk_recv.at[d - 1], (pb, (ka + d) % parts))
+                for d in range(1, parts)
+            ]
+            for copy in xk_copies:
+                copy.start()
+        if step == n // 2 - 2:
+            v_across.wait()
+            v_pass.start()
+            v_partner.wait()
+            for copy in xk_copies:
+                copy.wait()
+            xout_ref[...] = x_all[...]
+            v_pass.wait()
+
+            def split(p, carry):
+                for j in range(parts):
+                    high, low = halves(v_all[j, p])
+                    v_high[p, pl.ds(j * rows, rows), :] = high
+                    v_low[p, pl.ds(j * rows, rows), :] = low
+                return carry
+
+            lax.fori_loop(0, pairs, split, 0)
+            lax.fori_loop(0, n - 3, block, 0)
+        if step == n // 2 - 1:
+            lax.fori_loop(n - 3, n - 1, block, 0)
+    copies[0].wait()
+    copies[1].wait()
+    lax.fori_loop(n - 1, n, block, 0)
+
+    mine = pl.ds(pl.multiple_of(ka * rows, rows), rows)
+
+    def total(q, carry):
+        for d in range(1, parts):
+            k_copy(q, d).wait()
+        for s in range(capacity):
+            value = k_part[q, s, mine, :]
+            for d in range(1, parts):
+                value = value + k_in[d - 1, q, s]
+            k_ref[q, s] = value
+        return carry
+
+    lax.fori_loop(0, n, total, 0)
+
+
+def reduce_kernel(n, parts, y_ref, out_ref, landed, send_sem, recv_sem):
+    pb, ka = lax.axis_index("pb"), lax.axis_index("ka")
+    count = n * parts
+    me = pb * parts + ka
+    barrier = pltpu.get_barrier_semaphore()
+
+    def greet(d, carry):
+        to = (me + d) % count
+        pl.semaphore_signal(barrier, inc=1, device_id=(to // parts, to % parts), device_id_type=MESH)
+        return carry
+
+    lax.fori_loop(1, count, greet, 0)
+    pl.semaphore_wait(barrier, count - 1)
+
+    def copy(d):
+        to = (me + d) % count
+        return pltpu.make_async_remote_copy(
+            src_ref=y_ref.at[to], dst_ref=landed.at[d], send_sem=send_sem.at[d], recv_sem=recv_sem.at[d],
+            device_id=(to // parts, to % parts), device_id_type=MESH,
+        )
+
+    def send(d, carry):
+        copy(d).start()
+        return carry
+
+    lax.fori_loop(1, count, send, 0)
+
+    def take(d, total):
+        copy(d).wait()
+        return total + landed[d]
+
+    out_ref[...] = lax.fori_loop(1, count, take, y_ref[me])
+
+
+def ringed(valence, conduction, screened, momentum, kpairs, kpoint_slot, trial_blocks):
+    high = lax.Precision.HIGH
+    pair_dev, rows, waves = valence.shape
+    n, parts = lax.axis_size("pb"), lax.axis_size("ka")
+    capacity, slot_count, position, source = slots(momentum, pair_dev, n)
+    trials = trial_blocks.shape[1] // (VB * CB)
+    wide = VB * CB
+    depth = conduction.shape[2]
+    columns = conduction.shape[1]
+    vmem = pl.BlockSpec(memory_space=pltpu.VMEM)
+    any_space = pl.BlockSpec(memory_space=pl.ANY)
+    dma = pltpu.SemaphoreType.DMA
+    kernel, x_all = pl.pallas_call(
+        functools.partial(kernel_blocks_kernel, n, parts, capacity),
+        out_shape=(
+            jax.ShapeDtypeStruct((n, capacity, rows, columns), jnp.float32),
+            jax.ShapeDtypeStruct((parts, n, trials, wide), jnp.float32),
+        ),
+        in_specs=[pl.BlockSpec(memory_space=pltpu.SMEM), any_space, vmem, any_space, vmem],
+        out_specs=(vmem, vmem),
+        scratch_shapes=[
+            pltpu.VMEM((n, depth, waves), jnp.float32),
+            pltpu.VMEM((parts, pair_dev, rows, waves), jnp.float32),
+            pltpu.VMEM((pair_dev, parts * rows, waves), jnp.bfloat16),
+            pltpu.VMEM((pair_dev, parts * rows, waves), jnp.bfloat16),
+            pltpu.VMEM((capacity * parts * rows, waves), jnp.bfloat16),
+            pltpu.VMEM((capacity * parts * rows, waves), jnp.bfloat16),
+            pltpu.VMEM((n, capacity, parts * rows, columns), jnp.float32),
+            pltpu.VMEM((parts - 1, n, capacity, rows, columns), jnp.float32),
+            pltpu.VMEM((parts, n, trials, wide), jnp.float32),
+            dma((2,)), dma((3,)), dma((3,)), dma((n // 2, 2)), dma((n // 2, 2)),
+            dma((n, parts - 1)), dma((n, parts - 1)), dma((n - 1,)), dma((n - 1,)), dma((parts - 1,)), dma((parts - 1,)),
+        ],
+        compiler_params=pltpu.CompilerParams(collective_id=0, has_side_effects=True, vmem_limit_bytes=56 * 1024 * 1024),
+    )(source, valence, conduction, screened, trial_blocks.reshape(trials, wide))
+    ka = lax.axis_index("ka")
+    local_v = rows // VB
+    mine = jnp.take(kernel.reshape(slot_count, rows, columns), position, axis=0)
+    mixed = mine.reshape(pair_dev, local_v, VB, CB, CB).transpose(0, 1, 3, 2, 4).reshape(pair_dev, local_v * CB, wide)
+    blocks = x_all.transpose(1, 0, 2, 3).reshape(n, parts * trials, wide)
+    slot_near = jnp.take(kpoint_slot, kpairs[:, 0])
+    slot_far = jnp.take(kpoint_slot, kpairs[:, 1])
+    part = lax.dynamic_slice_in_dim(blocks, ka * local_v * CB, local_v * CB, axis=2)
+    far_trials = jnp.take(blocks, slot_far, axis=0)
+    near_trials = jnp.take(part, slot_near, axis=0)
+    direct = jnp.einsum("pam,pnm->pna", mixed, far_trials, precision=high, preferred_element_type=jnp.float32)
+    mirror = jnp.einsum("pam,pna->pnm", mixed, near_trials, precision=high, preferred_element_type=jnp.float32)
+    kpoint_rows = jnp.arange(n, dtype=jnp.int32)[:, None]
+    onehot_near = (slot_near[None, :] == kpoint_rows).astype(jnp.float32)
+    onehot_far = (slot_far[None, :] == kpoint_rows).astype(jnp.float32)
+    summed_near = jnp.einsum("kp,pna->kna", onehot_near, direct, precision=high, preferred_element_type=jnp.float32)
+    summed_far = jnp.einsum("kp,pnm->knm", onehot_far, mirror, precision=high, preferred_element_type=jnp.float32)
+    spread = lax.dynamic_update_slice_in_dim(jnp.zeros_like(summed_far), summed_near, ka * local_v * CB, axis=2)
+    contributions = (summed_far + spread).reshape(n * parts, trials, wide)
+    return reduced(n, parts, contributions).reshape(1, trials * wide)
+
+
+def reduced(n, parts, contributions):
+    count, trials, wide = contributions.shape
+    vmem = pl.BlockSpec(memory_space=pltpu.VMEM)
+    return pl.pallas_call(
+        functools.partial(reduce_kernel, n, parts),
+        out_shape=jax.ShapeDtypeStruct((trials, wide), jnp.float32),
+        in_specs=[vmem],
+        out_specs=vmem,
+        scratch_shapes=[
+            pltpu.VMEM((count, trials, wide), jnp.float32),
+            pltpu.SemaphoreType.DMA((count,)),
+            pltpu.SemaphoreType.DMA((count,)),
+        ],
+        compiler_params=pltpu.CompilerParams(collective_id=1, has_side_effects=True, vmem_limit_bytes=32 * 1024 * 1024),
+    )(contributions)
+
+
+def slots(momentum, pair_dev, owners):
+    capacity = max(2, 2 * pair_dev // owners)
+    slot_count = owners * capacity
+    target = momentum[:, 0]
+    indices = jnp.arange(pair_dev, dtype=jnp.int32)
+    earlier = (target[:, None] == target[None, :]) & (indices[None, :] < indices[:, None])
+    position = target * capacity + jnp.sum(earlier.astype(jnp.int32), axis=1)
+    matches = position[None, :] == jnp.arange(slot_count, dtype=jnp.int32)[:, None]
+    source = jnp.sum(jnp.where(matches, indices[None, :], 0), axis=1)
+    return capacity, slot_count, position, source
 
 
 def local(valence, conduction, screened, momentum, kpairs, kpoint_slot, trial_blocks):
+    n, parts = lax.axis_size("pb"), lax.axis_size("ka")
+    if n >= 8 and n % 2 == 0 and parts == 4 and n * conduction.shape[2] * valence.shape[2] * 4 <= 16 * 1024 * 1024:
+        return ringed(valence, conduction, screened, momentum, kpairs, kpoint_slot, trial_blocks)
+    return routed(valence, conduction, screened, momentum, kpairs, kpoint_slot, trial_blocks)
+
+
+def routed(valence, conduction, screened, momentum, kpairs, kpoint_slot, trial_blocks):
     highest = lax.Precision.HIGHEST
     pair_dev = valence.shape[0]
     owners = lax.axis_size("pb")

time: 677 us -> 136 us (0.20)
  waiting for transfers between devices: 346 us -> 0 us
  Pallas kernels: 0 us -> 112 us
  blocking collectives: 109 us -> 0 us
  local copies, waits for them, and re-layouts: 112 us -> 12.3 us
  matrix products: 63.7 us -> 4.34 us
  between operations: 13.8 us -> 0.2 us
  other arithmetic: 15.2 us -> 4.31 us
  starting transfers between devices: 9.63 us -> 0 us
    psum x1 -> x0, waiting for transfers between devices: 207 us -> none  [local(): kernel = lax.psum(partial_kernel, 'ka')]
    pallas_call x0 -> x2, Pallas kernels: none -> 112 us  [the longest x1 99.1 us: ringed(): pl.pallas_call(functools.partial(kernel_blocks_kernel, n, parts, capacity...]
    all_to_all x1 -> x0, blocking collectives: 78 us -> none  [local(): lax.all_to_all(outgoing, 'pb', split_axis=0, concat_axis=0, tiled=True)]
    all_to_all x2 -> x0, waiting for transfers between devices: 69.8 us -> none  [the longest x1 69.8 us: local(): lax.all_to_all(product, 'pb', split_axis=0, concat_axis=0, tiled=True)]
    unnamed x3 -> x0, waiting for transfers between devices: 68.9 us -> none
    dot_general x6 -> x4, matrix products: 63.7 us -> 4.34 us  [the longest x1 1.67 us: ringed(): jnp.einsum('pam,pna->pnm', mixed, near_trials, precision=high, preferred_...]
    all_gather x1 -> x0, blocking collectives: 30.6 us -> none  [local(): gathered = lax.all_gather(trial_blocks, 'pb', axis=0, tiled=True)]
    unnamed x20 -> x6, local copies, waits for them, and re-layouts: 29.1 us -> 0.01 us
  transfers between devices with their start and end apart: 4 -> 0, of which waited for: 3 -> 0; matrix products, arithmetic and copies ran while one was open for 1% -> 0% of each run, Pallas kernels for 0% -> 0%
where the time goes in v1:
time: 136 us; the launch traced here: 134 us
  Pallas kernels  112 us (82%)
  local copies, waits for them, and re-layouts  12.3 us (9%)
  matrix products  4.34 us (3%)
  other arithmetic  4.31 us (3%)
    pallas_call x1, Pallas kernels, ringed(): pl.pallas_call(functools.partial(kernel_blocks_kernel, n, parts, capacity...  99.1 us
    pallas_call x1, Pallas kernels, reduced(): pl.pallas_call(functools.partial(reduce_kernel, n, parts), out_shape=jax....  13.2 us
    transpose x1, local copies, waits for them, and re-layouts, ringed(): mine.reshape(pair_dev, local_v, VB, CB, CB).transpose(0, 1, 3, 2, 4)  3.07 us
    gather x2, local copies, waits for them, and re-layouts, ringed(): mine = jnp.take(kernel.reshape(slot_count, rows, columns), position, axis=0)  2.89 us

profile of v1, /device:TPU:0, one launch (start us, length us, event | category | flops | bytes accessed | tf_op | source)
XLA Modules:
  0.0 133.6 jit_solution(10113840169607043986)
XLA Ops:
  0.0 0.0 copy-start
  0.0 0.9 convert_reduce_fusion
  0.9 0.7 multiply_add_fusion
  1.6 0.6 select_reduce_fusion.source_ref
  2.2 0.8 reduce
  2.9 0.7 reshape.52.x_ref
  3.6 0.0 copy-start.2
  3.6 99.1 %shard_map.73 = (f32[8,6,16,196]{3,2,1,0:T(8,128)}, f32[4,8,32,112]{3,2,1,0:T(8,128)}) custom-call(s32[48]{0:T(128)} %select_reduce_fusion.source_ref, f32[26,16,1024]{2,1,0:T(8,128)} %v_ref.1, bf16[26,196,256]{2,1,0:T(8,128)(2,1)} %c_ref.1, f32[1,1024,1024]{2,1,0:T(8,128)} %w_ref.1, f32[32,112]{1,0:T(8,128)} %reshape.52.x_ref), custom_call_target="tpu_custom_call" | custom-call | tf_op jit(solution)/shard_map/pallas_call | solution.py:220
  102.8 0.0 copy-done.2
  102.8 1.7 %gather_fusion.1 = f32[26,16,196]{2,1,0:T(8,128)S(1)} fusion(f32[48,16,196]{2,1,0:T(8,128)} %bitcast.42, s32[1024]{0:T(1024)S(1)} %pad_clamp_fusion.1), kind=kCustom, calls=%fused_computation.3 | custom fusion | bytes 652392 | tf_op jit(solution)/shard_map/jit(_take)/gather | solution.py:245
  104.5 1.2 copy.21
  105.7 1.3 select_bitcast_fusion
  107.0 3.1 %copy.22 = f32[26,2,14,8,14]{4,3,2,1,0:T(8,128)S(1)} copy(f32[26,2,14,8,14]{0,3,1,4,2:T(8,128)} %select_bitcast_fusion) | data formatting | bytes 652288 | tf_op jit(solution)/shard_map/transpose | solution.py:246
  110.1 0.8 reshape.55
  110.9 0.0 copy-start.1
  110.9 1.1 copy.20
  112.0 0.2 constant_dynamic-slice_fusion
  112.2 0.0 copy-done.1
  112.2 0.0 copy-done
  112.2 0.7 gather_fusion.3
  112.9 0.7 gather_fusion.4
  113.7 0.7 gather_fusion
  114.4 1.7 %fusion.4 = f32[26,128,112]{1,2,0:T(8,128)S(1)} fusion(f32[26,28,112]{2,1,0:T(8,128)S(1)} %reshape.55, f32[26,128,28]{2,1,0:T(8,128)S(1)} %gather_fusion, pred[26]{0:T(512)(128)(4,1)S(1)} %get-tuple-element.16), kind=kOutput, calls=%fused_computation.9 | convolution fusion | flops 62712832 | bytes 2189850 | tf_op jit(solution)/shard_map/pam,pna->pnm/dot_general | solution.py:254
  116.0 0.8 fusion
  116.8 0.7 gather_fusion.2
  117.5 1.5 %fusion.2 = f32[26,128,28]{1,2,0:T(8,128)S(1)} fusion(f32[26,28,112]{2,1,0:T(8,128)S(1)} %reshape.55, f32[26,128,112]{2,1,0:T(8,128)S(1)} %gather_fusion.2, pred[26]{0:T(512)(128)(4,1)S(1)} %get-tuple-element.10), kind=kOutput, calls=%fused_computation.7 | convolution fusion | flops 62992384 | bytes 2189850 | tf_op jit(solution)/shard_map/pam,pnm->pna/dot_general | solution.py:253
  119.0 0.4 fusion.6
  119.4 0.2 copy.27
  119.6 13.2 %shard_map.74 = f32[32,112]{1,0:T(8,128)S(1)} custom-call(f32[32,32,112]{2,1,0:T(8,128)S(1)} %bitcast.37), custom_call_target="tpu_custom_call" | custom-call | tf_op jit(solution)/shard_map/pallas_call | solution.py:268
  132.9 0.7 reshape.57
  (9 shorter events, 0.1 us)
Async XLA Ops:
  0.0 112.2 %copy-start = (s32[8]{0:T(128)S(1)}, s32[8]{0:T(128)}, u32[]{:S(2)}) copy-start(s32[8]{0:T(128)} %param.14) | copy-start | bytes 100
  3.6 99.2 %copy-start.2 = (s32[26,1]{0,1:T(1,128)S(1)}, s32[26,1]{0,1:T(1,128)}, u32[]{:S(2)}) copy-start(s32[26,1]{0,1:T(1,128)} %param.12) | copy-start | bytes 316
  110.9 1.3 copy-start.1

commit v2 on v1

--- a/solution.py
+++ b/solution.py
@@ -30,7 +30,7 @@
     n, parts, capacity,
     source_ref, v_ref, c_ref, w_ref, x_ref,
     k_ref, xout_ref,
-    w_all, v_all, v_high, v_low, g_high, g_low, k_part, k_in, x_all,
+    w_all, v_all, v_high, v_low, stacked, rows_of, k_part, k_in, x_all,
     local_sems, v_send, v_recv, ring_send, ring_recv, k_send, k_recv, x_send, x_recv, xk_send, xk_recv,
 ):
     pb, ka = lax.axis_index("pb"), lax.axis_index("ka")
@@ -88,32 +88,65 @@
     for copy in x_copies:
         copy.start()
 
+    two = 2 * rows
+    span = capacity * two
+    chip = ka - ka % 2
+    other = (chip + 2) % parts
+
+    def split(side):
+        base = chip if side == 0 else other
+
+        def one(p, carry):
+            for j in range(2):
+                high, low = halves(v_all[base + j, p])
+                v_high[side, p, pl.ds(j * rows, rows), :] = high
+                v_low[side, p, pl.ds(j * rows, rows), :] = low
+            return carry
+
+        lax.fori_loop(0, pairs, one, 0)
+
     def k_copy(q, d):
-        to = (ka + d) % parts
+        if d == 0:
+            to, at = partner, (1 - ka % 2) * rows
+        elif d == 1:
+            to, at = across, two + (ka % 2) * rows
+        else:
+            to, at = (partner + 2) % parts, two + (1 - ka % 2) * rows
         return remote(
-            k_part.at[q, :, pl.ds(pl.multiple_of(to * rows, rows), rows), :],
-            k_in.at[d - 1, q],
-            k_send.at[q, d - 1], k_recv.at[q, d - 1], (pb, to),
+            k_part.at[q, :, pl.ds(pl.multiple_of(at, rows), rows), :], k_in.at[d, q], k_send.at[q, d], k_recv.at[q, d], (pb, to)
         )
 
-    def block(k, carry):
-        at = (place + n + ((k + 1) // 2) * (2 * (k % 2) - 1)) % n
-        q = ring_index(at, n)
-        high, low = halves(w_all[at])
-        for s in range(capacity):
-            p = source_ref[q * capacity + s]
-            g_high[pl.ds(s * parts * rows, parts * rows), :] = v_high[p]
-            g_low[pl.ds(s * parts * rows, parts * rows), :] = v_low[p]
-        screened = dot_nt(g_high[...], high) + (dot_nt(g_high[...], low) + dot_nt(g_low[...], high))
-        s_high, s_low = halves(screened)
-        for s in range(capacity):
-            span = slice(s * parts * rows, (s + 1) * parts * rows)
-            conduct = c_ref[source_ref[q * capacity + s]]
-            k_part[q, s] = dot_nt(s_high[span], conduct) + dot_nt(s_low[span], conduct)
-        for d in range(1, parts):
-            k_copy(q, d).start()
-        return carry
-
+    def place_of(k):
+        return (place + n + ((k + 1) // 2) * (2 * (k % 2) - 1)) % n
+
+    def screen(side, first, last):
+        def block(k, carry):
+            at = place_of(k)
+            q = ring_index(at, n)
+            high, low = halves(w_all[at])
+            for s in range(capacity):
+                p = source_ref[q * capacity + s]
+                stacked[pl.ds(s * two, two), :] = v_high[side, p]
+                stacked[pl.ds(span + s * two, two), :] = v_low[side, p]
+            both = dot_nt(stacked[...], high)
+            screened = both[:span] + (both[span:] + dot_nt(stacked[pl.ds(0, span), :], low))
+            s_high, s_low = halves(screened)
+            for s in range(capacity):
+                rows_of[at, s, pl.ds(side * two, two), :] = s_high[s * two:(s + 1) * two]
+                rows_of[at, s, pl.ds(2 * two + side * two, two), :] = s_low[s * two:(s + 1) * two]
+            if side == 1:
+                for s in range(capacity):
+                    both = dot_nt(rows_of[at, s], c_ref[source_ref[q * capacity + s]])
+                    k_part[q, s] = both[:2 * two] + both[2 * two:]
+                for d in range(parts - 1):
+                    k_copy(q, d).start()
+            return carry
+
+        lax.fori_loop(first, last, block, 0)
+
+    v_partner.wait()
+    split(0)
+    screen(0, 0, 1)
     for step in range(1, n // 2):
         later = ring(step)
         copies[0].wait_recv()
@@ -132,81 +165,160 @@
             ]
             for copy in xk_copies:
                 copy.start()
-        if step == n // 2 - 2:
+        if step < n // 2 - 2:
+            screen(0, 2 * step - 1, 2 * step + 1)
+        if step == n // 2 - 3:
             v_across.wait()
             v_pass.start()
-            v_partner.wait()
+        if step == n // 2 - 2:
+            v_pass.wait()
+            split(1)
+            screen(1, 0, n - 5)
+            screen(0, n - 5, n - 3)
             for copy in xk_copies:
                 copy.wait()
             xout_ref[...] = x_all[...]
-            v_pass.wait()
-
-            def split(p, carry):
-                for j in range(parts):
-                    high, low = halves(v_all[j, p])
-                    v_high[p, pl.ds(j * rows, rows), :] = high
-                    v_low[p, pl.ds(j * rows, rows), :] = low
-                return carry
-
-            lax.fori_loop(0, pairs, split, 0)
-            lax.fori_loop(0, n - 3, block, 0)
         if step == n // 2 - 1:
-            lax.fori_loop(n - 3, n - 1, block, 0)
+            screen(1, n - 5, n - 3)
+            screen(0, n - 3, n - 1)
+            screen(1, n - 3, n - 1)
     copies[0].wait()
     copies[1].wait()
-    lax.fori_loop(n - 1, n, block, 0)
-
-    mine = pl.ds(pl.multiple_of(ka * rows, rows), rows)
+    screen(0, n - 1, n)
+    screen(1, n - 1, n)
+
+    mine = pl.ds(pl.multiple_of((ka % 2) * rows, rows), rows)
 
     def total(q, carry):
-        for d in range(1, parts):
+        for d in range(parts - 1):
             k_copy(q, d).wait()
         for s in range(capacity):
-            value = k_part[q, s, mine, :]
-            for d in range(1, parts):
-                value = value + k_in[d - 1, q, s]
-            k_ref[q, s] = value
+            k_ref[q, s] = k_part[q, s, mine, :] + (k_in[0, q, s] + (k_in[1, q, s] + k_in[2, q, s]))
         return carry
 
     lax.fori_loop(0, n, total, 0)
 
 
-def reduce_kernel(n, parts, y_ref, out_ref, landed, send_sem, recv_sem):
+def response_kernel(
+    n, parts,
+    position_ref, near_ref, far_ref, k_ref, x_ref, mask_ref, spread_ref, put_ref,
+    out_ref,
+    wide_rows, mixed, m_high, m_low, x_stack, x_part, direct, mirror, given, landed, joined, landed_pb,
+    ka_send, ka_recv, pb_send, pb_recv,
+):
     pb, ka = lax.axis_index("pb"), lax.axis_index("ka")
-    count = n * parts
-    me = pb * parts + ka
+    pairs = direct.shape[0]
+    trials, wide = out_ref.shape
+    every = parts * trials
+    band = put_ref.shape[0]
+    local_v = k_ref.shape[1] // VB
+    tall = band // local_v
     barrier = pltpu.get_barrier_semaphore()
-
-    def greet(d, carry):
-        to = (me + d) % count
-        pl.semaphore_signal(barrier, inc=1, device_id=(to // parts, to % parts), device_id_type=MESH)
-        return carry
-
-    lax.fori_loop(1, count, greet, 0)
-    pl.semaphore_wait(barrier, count - 1)
-
-    def copy(d):
-        to = (me + d) % count
-        return pltpu.make_async_remote_copy(
-            src_ref=y_ref.at[to], dst_ref=landed.at[d], send_sem=send_sem.at[d], recv_sem=recv_sem.at[d],
-            device_id=(to // parts, to % parts), device_id_type=MESH,
-        )
-
-    def send(d, carry):
-        copy(d).start()
-        return carry
-
-    lax.fori_loop(1, count, send, 0)
-
-    def take(d, total):
-        copy(d).wait()
-        return total + landed[d]
-
-    out_ref[...] = lax.fori_loop(1, count, take, y_ref[me])
+    for d in range(1, n):
+        pl.semaphore_signal(barrier, inc=1, device_id=((pb + d) % n, ka), device_id_type=MESH)
+    for d in range(1, parts):
+        pl.semaphore_signal(barrier, inc=1, device_id=(pb, (ka + d) % parts), device_id_type=MESH)
+
+    def dot(a, b):
+        return jnp.dot(a, b, preferred_element_type=jnp.float32)
+
+    for w in range(VB):
+        def fill(p, carry):
+            values = k_ref[position_ref[p]]
+            for v in range(local_v):
+                row = values[v * VB + w:v * VB + w + 1]
+                high, low = halves(jnp.broadcast_to(row, mask_ref.shape) * mask_ref[...])
+                wide_rows[0, p, pl.ds(v * tall, tall), :] = high
+                wide_rows[1, p, pl.ds(v * tall, tall), :] = low
+            return carry
+
+        lax.fori_loop(0, pairs, fill, 0)
+        lanes = wide_rows.shape[-1]
+        part = dot(wide_rows[...].reshape(2 * pairs * band, lanes), spread_ref[w])
+        if w == 0:
+            mixed[...] = part
+        else:
+            mixed[...] += part
+
+    def cut(p, carry):
+        value = mixed[pl.ds(pl.multiple_of(p * band, band), band), :]
+        value = value + mixed[pl.ds(pl.multiple_of((pairs + p) * band, band), band), :]
+        high, low = halves(value)
+        m_high[p] = high
+        m_low[p] = low
+        return carry
+
+    lax.fori_loop(0, pairs, cut, 0)
+
+    def trial(m, carry):
+        for j in range(parts):
+            high, low = halves(x_ref[j, m])
+            x_stack[m, pl.ds(j * trials, trials), :] = high
+            x_stack[m, pl.ds(every + j * trials, trials), :] = low
+        x_part[m] = dot_nt(x_stack[m], put_ref[...]).astype(jnp.bfloat16)
+        return carry
+
+    lax.fori_loop(0, n, trial, 0)
+
+    def pair(p, carry):
+        far = x_stack[far_ref[p]]
+        both = dot_nt(far, m_high[p])
+        direct[p] = both[:every] + (both[every:] + dot_nt(far[:every], m_low[p]))
+        near = x_part[near_ref[p]]
+        both = dot(near, m_high[p])
+        mirror[p] = both[:every] + (both[every:] + dot(near[:every], m_low[p]))
+        return carry
+
+    lax.fori_loop(0, pairs, pair, 0)
+    pl.semaphore_wait(barrier, n + parts - 2)
+
+    def remote(src, dst, send, recv, to):
+        return pltpu.make_async_remote_copy(src_ref=src, dst_ref=dst, send_sem=send, recv_sem=recv, device_id=to, device_id_type=MESH)
+
+    def ka_copy(m, d):
+        to = (ka + d) % parts
+        return remote(given.at[m, to], landed.at[d - 1, m], ka_send.at[m, d - 1], ka_recv.at[m, d - 1], (pb, to))
+
+    def pb_copy(d):
+        to = (pb + d) % n
+        return remote(joined.at[to], landed_pb.at[d - 1], pb_send.at[d - 1], pb_recv.at[d - 1], (to, ka))
+
+    def gather(m, carry):
+        def add(ref, index_ref):
+            def step(p, total):
+                return total + ref[p] * (index_ref[p] == m).astype(jnp.float32)
+
+            return lax.fori_loop(0, pairs, step, jnp.zeros(ref.shape[1:], jnp.float32))
+
+        high, low = halves(add(direct, near_ref))
+        value = add(mirror, far_ref) + (dot(high, put_ref[...]) + dot(low, put_ref[...]))
+        for j in range(parts):
+            given[m, j] = value[j * trials:(j + 1) * trials]
+        for d in range(1, parts):
+            ka_copy(m, d).start()
+        return carry
+
+    lax.fori_loop(0, n, gather, 0)
+
+    def join(m, carry):
+        value = given[m, ka]
+        for d in range(1, parts):
+            ka_copy(m, d).wait()
+            value = value + landed[d - 1, m]
+        joined[m] = value
+        return carry
+
+    lax.fori_loop(0, n, join, 0)
+    for d in range(1, n):
+        pb_copy(d).start()
+    value = joined[pb]
+    for d in range(1, n):
+        pb_copy(d).wait()
+        value = value + landed_pb[d - 1]
+    out_ref[...] = value
 
 
 def ringed(valence, conduction, screened, momentum, kpairs, kpoint_slot, trial_blocks):
-    high = lax.Precision.HIGH
     pair_dev, rows, waves = valence.shape
     n, parts = lax.axis_size("pb"), lax.axis_size("ka")
     capacity, slot_count, position, source = slots(momentum, pair_dev, n)
@@ -228,10 +340,10 @@
         scratch_shapes=[
             pltpu.VMEM((n, depth, waves), jnp.float32),
             pltpu.VMEM((parts, pair_dev, rows, waves), jnp.float32),
-            pltpu.VMEM((pair_dev, parts * rows, waves), jnp.bfloat16),
-            pltpu.VMEM((pair_dev, parts * rows, waves), jnp.bfloat16),
-            pltpu.VMEM((capacity * parts * rows, waves), jnp.bfloat16),
-            pltpu.VMEM((capacity * parts * rows, waves), jnp.bfloat16),
+            pltpu.VMEM((2, pair_dev, 2 * rows, waves), jnp.bfloat16),
+            pltpu.VMEM((2, pair_dev, 2 * rows, waves), jnp.bfloat16),
+            pltpu.VMEM((capacity * 4 * rows, waves), jnp.bfloat16),
+            pltpu.VMEM((n, capacity, 8 * rows, depth), jnp.bfloat16),
             pltpu.VMEM((n, capacity, parts * rows, columns), jnp.float32),
             pltpu.VMEM((parts - 1, n, capacity, rows, columns), jnp.float32),
             pltpu.VMEM((parts, n, trials, wide), jnp.float32),
@@ -242,41 +354,43 @@
     )(source, valence, conduction, screened, trial_blocks.reshape(trials, wide))
     ka = lax.axis_index("ka")
     local_v = rows // VB
-    mine = jnp.take(kernel.reshape(slot_count, rows, columns), position, axis=0)
-    mixed = mine.reshape(pair_dev, local_v, VB, CB, CB).transpose(0, 1, 3, 2, 4).reshape(pair_dev, local_v * CB, wide)
-    blocks = x_all.transpose(1, 0, 2, 3).reshape(n, parts * trials, wide)
-    slot_near = jnp.take(kpoint_slot, kpairs[:, 0])
-    slot_far = jnp.take(kpoint_slot, kpairs[:, 1])
-    part = lax.dynamic_slice_in_dim(blocks, ka * local_v * CB, local_v * CB, axis=2)
-    far_trials = jnp.take(blocks, slot_far, axis=0)
-    near_trials = jnp.take(part, slot_near, axis=0)
-    direct = jnp.einsum("pam,pnm->pna", mixed, far_trials, precision=high, preferred_element_type=jnp.float32)
-    mirror = jnp.einsum("pam,pna->pnm", mixed, near_trials, precision=high, preferred_element_type=jnp.float32)
-    kpoint_rows = jnp.arange(n, dtype=jnp.int32)[:, None]
-    onehot_near = (slot_near[None, :] == kpoint_rows).astype(jnp.float32)
-    onehot_far = (slot_far[None, :] == kpoint_rows).astype(jnp.float32)
-    summed_near = jnp.einsum("kp,pna->kna", onehot_near, direct, precision=high, preferred_element_type=jnp.float32)
-    summed_far = jnp.einsum("kp,pnm->knm", onehot_far, mirror, precision=high, preferred_element_type=jnp.float32)
-    spread = lax.dynamic_update_slice_in_dim(jnp.zeros_like(summed_far), summed_near, ka * local_v * CB, axis=2)
-    contributions = (summed_far + spread).reshape(n * parts, trials, wide)
-    return reduced(n, parts, contributions).reshape(1, trials * wide)
-
-
-def reduced(n, parts, contributions):
-    count, trials, wide = contributions.shape
-    vmem = pl.BlockSpec(memory_space=pltpu.VMEM)
-    return pl.pallas_call(
-        functools.partial(reduce_kernel, n, parts),
+    tall = -(-CB // 16) * 16
+    band = local_v * tall
+    every = parts * trials
+    c_of, d_of = jnp.arange(columns, dtype=jnp.int32) // CB, jnp.arange(columns, dtype=jnp.int32) % CB
+    mask = (jnp.arange(tall, dtype=jnp.int32)[:, None] == c_of[None, :]).astype(jnp.float32)
+    w_to, d_to = jnp.arange(wide, dtype=jnp.int32) // CB, jnp.arange(wide, dtype=jnp.int32) % CB
+    same_d = d_of[:, None] == d_to[None, :]
+    spread = (same_d[None] & (w_to[None, None, :] == jnp.arange(VB, dtype=jnp.int32)[:, None, None])).astype(jnp.bfloat16)
+    v_row, c_row = jnp.arange(band, dtype=jnp.int32) // tall, jnp.arange(band, dtype=jnp.int32) % tall
+    put = ((ka * local_v + v_row)[:, None] == w_to[None, :]) & (c_row[:, None] == d_to[None, :])
+    smem = pl.BlockSpec(memory_space=pltpu.SMEM)
+    result = pl.pallas_call(
+        functools.partial(response_kernel, n, parts),
         out_shape=jax.ShapeDtypeStruct((trials, wide), jnp.float32),
-        in_specs=[vmem],
+        in_specs=[smem] * 3 + [vmem] * 5,
         out_specs=vmem,
         scratch_shapes=[
-            pltpu.VMEM((count, trials, wide), jnp.float32),
-            pltpu.SemaphoreType.DMA((count,)),
-            pltpu.SemaphoreType.DMA((count,)),
+            pltpu.VMEM((2, pair_dev, band, columns), jnp.bfloat16),
+            pltpu.VMEM((2 * pair_dev * band, wide), jnp.float32),
+            pltpu.VMEM((pair_dev, band, wide), jnp.bfloat16),
+            pltpu.VMEM((pair_dev, band, wide), jnp.bfloat16),
+            pltpu.VMEM((n, 2 * every, wide), jnp.bfloat16),
+            pltpu.VMEM((n, 2 * every, band), jnp.bfloat16),
+            pltpu.VMEM((pair_dev, every, band), jnp.float32),
+            pltpu.VMEM((pair_dev, every, wide), jnp.float32),
+            pltpu.VMEM((n, parts, trials, wide), jnp.float32),
+            pltpu.VMEM((parts - 1, n, trials, wide), jnp.float32),
+            pltpu.VMEM((n, trials, wide), jnp.float32),
+            pltpu.VMEM((n - 1, trials, wide), jnp.float32),
+            dma((n, parts - 1)), dma((n, parts - 1)), dma((n - 1,)), dma((n - 1,)),
         ],
-        compiler_params=pltpu.CompilerParams(collective_id=1, has_side_effects=True, vmem_limit_bytes=32 * 1024 * 1024),
-    )(contributions)
+        compiler_params=pltpu.CompilerParams(collective_id=1, has_side_effects=True, vmem_limit_bytes=48 * 1024 * 1024),
+    )(
+        position, jnp.take(kpoint_slot, kpairs[:, 0]), jnp.take(kpoint_slot, kpairs[:, 1]),
+        kernel.reshape(slot_count, rows, columns), x_all, mask, spread, put.astype(jnp.bfloat16),
+    )
+    return result.reshape(1, trials * wide)
 
 
 def slots(momentum, pair_dev, owners):

time: 136 us -> 143 us (1.051); the launches traced: 134 us -> 143 us
  Pallas kernels: 112 us -> 133 us
  local copies, waits for them, and re-layouts: 12.3 us -> 4.94 us
  matrix products: 4.34 us -> 0 us
    pallas_call x1, Pallas kernels: 13.2 us -> 30.3 us  [ringed(): pl.pallas_call(functools.partial(response_kernel, n, parts), out_shape=ja...]
    dot_general x4 -> x0, matrix products: 4.34 us -> none  [the longest x1 1.67 us: ringed(): jnp.einsum('pam,pna->pnm', mixed, near_trials, precision=high, preferred_...]
    gather x6 -> x2, local copies, waits for them, and re-layouts: 5.6 us -> 1.4 us  [the longest x1 0.7 us: ringed(): jnp.take(kpoint_slot, kpairs[:, 1])]
    transpose x2 -> x0, local copies, waits for them, and re-layouts: 4.15 us -> none  [the longest x1 3.07 us: ringed(): mine.reshape(pair_dev, local_v, VB, CB, CB).transpose(0, 1, 3, 2, 4)]
    pallas_call x1, Pallas kernels: 99.1 us -> 103 us  [ringed(): pl.pallas_call(functools.partial(kernel_blocks_kernel, n, parts, capacity...]
    unnamed x6, local copies, waits for them, and re-layouts: 0.01 us -> 2.17 us
    select_n x2 -> x6, other arithmetic: 0.01 us -> 1.57 us  [the longest x2 1.53 us: ringed(): jnp.take(kpoint_slot, kpairs[:, 1])]
where the time goes in v2:
time: 143 us
  Pallas kernels  133 us (93%)
  local copies, waits for them, and re-layouts  4.94 us (3%)
  other arithmetic  4.77 us (3%)
    pallas_call x1, Pallas kernels, ringed(): pl.pallas_call(functools.partial(kernel_blocks_kernel, n, parts, capacity...  103 us
    pallas_call x1, Pallas kernels, ringed(): pl.pallas_call(functools.partial(response_kernel, n, parts), out_shape=ja...  30.3 us

profile of v2, /device:TPU:0, one launch (start us, length us, event | category | flops | bytes accessed | tf_op | source)
XLA Modules:
  0.0 142.7 jit_solution(12838675698153391950)
XLA Ops:
  0.0 0.0 copy-start
  0.0 0.8 compare_select_fusion
  0.8 0.0 copy-done
  0.8 0.7 gather_fusion
  1.5 0.7 gather_fusion.1
  2.2 0.8 and_select_fusion
  3.0 0.1 and_convert_fusion.1.put_ref
  3.1 0.1 broadcast_compare_fusion
  3.2 0.1 and_convert_fusion.spread_ref
  3.3 0.9 convert_reduce_fusion
  4.2 0.7 multiply_add_fusion.position_ref
  4.9 0.6 select_reduce_fusion.source_ref
  5.5 0.8 reduce
  6.2 0.7 reshape.150.x_ref
  6.9 102.6 %shard_map.73 = (f32[8,6,16,196]{3,2,1,0:T(8,128)}, f32[4,8,32,112]{3,2,1,0:T(8,128)}) custom-call(s32[48]{0:T(128)} %select_reduce_fusion.source_ref, f32[26,16,1024]{2,1,0:T(8,128)} %v_ref.1, bf16[26,196,256]{2,1,0:T(8,128)(2,1)} %c_ref.1, f32[1,1024,1024]{2,1,0:T(8,128)} %w_ref.1, f32[32,112]{1,0:T(8,128)} %reshape.150.x_ref), custom_call_target="tpu_custom_call" | custom-call | tf_op jit(solution)/shard_map/pallas_call | solution.py:332
  109.5 0.0 copy-start.1
  109.5 1.1 copy-done.1
  110.6 0.0 copy-start.2
  110.6 1.0 copy-done.2
  111.7 30.3 %shard_map.74 = f32[32,112]{1,0:T(8,128)S(1)} custom-call(s32[26]{0:T(128)S(1)} %multiply_add_fusion.position_ref, s32[26]{0:T(128)S(1)} %get-tuple-element.11.near_ref, s32[26]{0:T(128)S(1)} %get-tuple-element.10.far_ref, f32[48,16,196]{2,1,0:T(8,128)S(1)} %bitcast.11, f32[4,8,32,112]{3,2,1,0:T(8,128)S(1)} %copy-done.2, f32[16,196]{1,0:T(8,128)S(1)} %fusion.1.mask_ref, ...), custom_call_target="tpu_custom_call" | custom-call | tf_op jit(solution)/shard_map/pallas_call | solution.py:368
  142.0 0.7 reshape.152
  (7 shorter events, 0.1 us)
Async XLA Ops:
  0.0 0.8 copy-start
  109.5 1.1 copy-start.1
  110.6 1.0 copy-start.2

commit v3 on v2

--- a/solution.py
+++ b/solution.py
@@ -2,6 +2,7 @@
 
 import jax
 import jax.numpy as jnp
+import numpy as np
 from jax import lax
 from jax.experimental import pallas as pl
 from jax.experimental.pallas import tpu as pltpu
@@ -201,18 +202,18 @@
 
 def response_kernel(
     n, parts,
-    position_ref, near_ref, far_ref, k_ref, x_ref, mask_ref, spread_ref, put_ref,
+    position_ref, far_ref, k_ref, x_ref, mask_ref, spread_ref, near_ref, pick_ref,
     out_ref,
-    wide_rows, mixed, m_high, m_low, x_stack, x_part, direct, mirror, given, landed, joined, landed_pb,
+    wide_rows, mixed, by_far, x_high, x_low, given, landed, joined, landed_pb,
     ka_send, ka_recv, pb_send, pb_recv,
 ):
     pb, ka = lax.axis_index("pb"), lax.axis_index("ka")
-    pairs = direct.shape[0]
-    trials, wide = out_ref.shape
-    every = parts * trials
-    band = put_ref.shape[0]
+    trials, wide = x_ref.shape[2:]
+    full = spread_ref.shape[2]
+    tall = mask_ref.shape[0]
     local_v = k_ref.shape[1] // VB
-    tall = band // local_v
+    band = local_v * tall
+    pairs = position_ref.shape[0]
     barrier = pltpu.get_barrier_semaphore()
     for d in range(1, n):
         pl.semaphore_signal(barrier, inc=1, device_id=((pb + d) % n, ka), device_id_type=MESH)
@@ -222,54 +223,54 @@
     def dot(a, b):
         return jnp.dot(a, b, preferred_element_type=jnp.float32)
 
-    for w in range(VB):
-        def fill(p, carry):
-            values = k_ref[position_ref[p]]
+    x_high[...] = jnp.zeros_like(x_high)
+    x_low[...] = jnp.zeros_like(x_low)
+    for m in range(n):
+        for j in range(parts):
+            high, low = halves(x_ref[j, m])
+            x_high[pl.ds(j * trials, trials), pl.ds(m * full, wide)] = high
+            x_low[pl.ds(j * trials, trials), pl.ds(m * full, wide)] = low
+
+    def fill(p, carry):
+        values = k_ref[position_ref[p]]
+        for w in range(VB):
             for v in range(local_v):
                 row = values[v * VB + w:v * VB + w + 1]
                 high, low = halves(jnp.broadcast_to(row, mask_ref.shape) * mask_ref[...])
-                wide_rows[0, p, pl.ds(v * tall, tall), :] = high
-                wide_rows[1, p, pl.ds(v * tall, tall), :] = low
-            return carry
-
-        lax.fori_loop(0, pairs, fill, 0)
-        lanes = wide_rows.shape[-1]
-        part = dot(wide_rows[...].reshape(2 * pairs * band, lanes), spread_ref[w])
+                wide_rows[w, p, pl.ds(v * tall, tall), :] = high
+                wide_rows[w, pairs + p, pl.ds(v * tall, tall), :] = low
+        return carry
+
+    lax.fori_loop(0, pairs, fill, 0)
+    lanes = wide_rows.shape[-1]
+    for w in range(VB):
+        part = dot(wide_rows[w].reshape(2 * pairs * band, lanes), spread_ref[w])
         if w == 0:
             mixed[...] = part
         else:
             mixed[...] += part
 
     def cut(p, carry):
-        value = mixed[pl.ds(pl.multiple_of(p * band, band), band), :]
-        value = value + mixed[pl.ds(pl.multiple_of((pairs + p) * band, band), band), :]
-        high, low = halves(value)
-        m_high[p] = high
-        m_low[p] = low
+        at = pl.multiple_of(p * band, band)
+        value = mixed[pl.ds(at, band), :] + mixed[pl.ds(pl.multiple_of((pairs + p) * band, band), band), :]
+        for m in range(n):
+            high, low = halves(value * (far_ref[p] == m).astype(jnp.float32))
+            by_far[0, pl.ds(at, band), pl.ds(m * full, full)] = high
+            by_far[1, pl.ds(at, band), pl.ds(m * full, full)] = low
         return carry
 
     lax.fori_loop(0, pairs, cut, 0)
-
-    def trial(m, carry):
+    g_high, g_low = halves(dot(near_ref[...], by_far[0]) + dot(near_ref[...], by_far[1]))
+    pick = pick_ref[...]
+    p_high = dot_nt(x_high[...], pick).astype(jnp.bfloat16)
+    p_low = dot_nt(x_low[...], pick).astype(jnp.bfloat16)
+    direct = dot_nt(x_high[...], g_high) + (dot_nt(x_high[...], g_low) + dot_nt(x_low[...], g_high))
+    d_high, d_low = halves(direct)
+    value = dot(p_high, g_high) + (dot(p_high, g_low) + dot(p_low, g_high))
+    value = value + (dot(d_high, pick) + dot(d_low, pick))
+    for m in range(n):
         for j in range(parts):
-            high, low = halves(x_ref[j, m])
-            x_stack[m, pl.ds(j * trials, trials), :] = high
-            x_stack[m, pl.ds(every + j * trials, trials), :] = low
-        x_part[m] = dot_nt(x_stack[m], put_ref[...]).astype(jnp.bfloat16)
-        return carry
-
-    lax.fori_loop(0, n, trial, 0)
-
-    def pair(p, carry):
-        far = x_stack[far_ref[p]]
-        both = dot_nt(far, m_high[p])
-        direct[p] = both[:every] + (both[every:] + dot_nt(far[:every], m_low[p]))
-        near = x_part[near_ref[p]]
-        both = dot(near, m_high[p])
-        mirror[p] = both[:every] + (both[every:] + dot(near[:every], m_low[p]))
-        return carry
-
-    lax.fori_loop(0, pairs, pair, 0)
+            given[m, j] = value[j * trials:(j + 1) * trials, m * full:(m + 1) * full]
     pl.semaphore_wait(barrier, n + parts - 2)
 
     def remote(src, dst, send, recv, to):
@@ -283,22 +284,12 @@
         to = (pb + d) % n
         return remote(joined.at[to], landed_pb.at[d - 1], pb_send.at[d - 1], pb_recv.at[d - 1], (to, ka))
 
-    def gather(m, carry):
-        def add(ref, index_ref):
-            def step(p, total):
-                return total + ref[p] * (index_ref[p] == m).astype(jnp.float32)
-
-            return lax.fori_loop(0, pairs, step, jnp.zeros(ref.shape[1:], jnp.float32))
-
-        high, low = halves(add(direct, near_ref))
-        value = add(mirror, far_ref) + (dot(high, put_ref[...]) + dot(low, put_ref[...]))
-        for j in range(parts):
-            given[m, j] = value[j * trials:(j + 1) * trials]
+    def send(m, carry):
         for d in range(1, parts):
             ka_copy(m, d).start()
         return carry
 
-    lax.fori_loop(0, n, gather, 0)
+    lax.fori_loop(0, n, send, 0)
 
     def join(m, carry):
         value = given[m, ka]
@@ -315,7 +306,7 @@
     for d in range(1, n):
         pb_copy(d).wait()
         value = value + landed_pb[d - 1]
-    out_ref[...] = value
+    out_ref[...] = value[:, :wide]
 
 
 def ringed(valence, conduction, screened, momentum, kpairs, kpoint_slot, trial_blocks):
@@ -357,38 +348,46 @@
     tall = -(-CB // 16) * 16
     band = local_v * tall
     every = parts * trials
-    c_of, d_of = jnp.arange(columns, dtype=jnp.int32) // CB, jnp.arange(columns, dtype=jnp.int32) % CB
-    mask = (jnp.arange(tall, dtype=jnp.int32)[:, None] == c_of[None, :]).astype(jnp.float32)
-    w_to, d_to = jnp.arange(wide, dtype=jnp.int32) // CB, jnp.arange(wide, dtype=jnp.int32) % CB
-    same_d = d_of[:, None] == d_to[None, :]
-    spread = (same_d[None] & (w_to[None, None, :] == jnp.arange(VB, dtype=jnp.int32)[:, None, None])).astype(jnp.bfloat16)
-    v_row, c_row = jnp.arange(band, dtype=jnp.int32) // tall, jnp.arange(band, dtype=jnp.int32) % tall
-    put = ((ka * local_v + v_row)[:, None] == w_to[None, :]) & (c_row[:, None] == d_to[None, :])
+    full = -(-wide // 128) * 128
+    c_of, d_of = np.arange(columns) // CB, np.arange(columns) % CB
+    lane = np.arange(full)
+    w_to, d_to = lane // CB, lane % CB
+    mask = (np.arange(tall)[:, None] == c_of[None, :]).astype(np.float32)
+    at_w = (w_to[None, None, :] == np.arange(VB)[:, None, None]) & (lane < wide)[None, None, :]
+    spread = ((d_of[:, None] == d_to[None, :])[None] & at_w).astype(jnp.bfloat16)
+    band_row = np.arange(n * band)
+    k_row, v_row, c_row = band_row // band, band_row % band // tall, band_row % tall
+    all_lane = np.arange(n * full)
+    same_c = (k_row[:, None] == all_lane[None, :] // full) & (c_row[:, None] == all_lane[None, :] % full % CB)
+    lane_v = np.where(all_lane % full < wide, all_lane % full // CB, -1).astype(np.int32)
+    pick = jnp.where(jnp.asarray(same_c) & ((ka * local_v + jnp.asarray(v_row, jnp.int32))[:, None] == jnp.asarray(lane_v)[None, :]), 1.0, 0.0)
+    pair_row = np.arange(pair_dev * band)
+    same_row = band_row[:, None] % band == pair_row[None, :] % band
+    slot_near = jnp.take(kpoint_slot, kpairs[:, 0])
+    near_lane = jnp.repeat(slot_near, band)
+    near = jnp.where(jnp.asarray(same_row) & (near_lane[None, :] == jnp.asarray(k_row, jnp.int32)[:, None]), 1.0, 0.0)
     smem = pl.BlockSpec(memory_space=pltpu.SMEM)
     result = pl.pallas_call(
         functools.partial(response_kernel, n, parts),
         out_shape=jax.ShapeDtypeStruct((trials, wide), jnp.float32),
-        in_specs=[smem] * 3 + [vmem] * 5,
+        in_specs=[smem] * 2 + [vmem] * 6,
         out_specs=vmem,
         scratch_shapes=[
-            pltpu.VMEM((2, pair_dev, band, columns), jnp.bfloat16),
-            pltpu.VMEM((2 * pair_dev * band, wide), jnp.float32),
-            pltpu.VMEM((pair_dev, band, wide), jnp.bfloat16),
-            pltpu.VMEM((pair_dev, band, wide), jnp.bfloat16),
-            pltpu.VMEM((n, 2 * every, wide), jnp.bfloat16),
-            pltpu.VMEM((n, 2 * every, band), jnp.bfloat16),
-            pltpu.VMEM((pair_dev, every, band), jnp.float32),
-            pltpu.VMEM((pair_dev, every, wide), jnp.float32),
-            pltpu.VMEM((n, parts, trials, wide), jnp.float32),
-            pltpu.VMEM((parts - 1, n, trials, wide), jnp.float32),
-            pltpu.VMEM((n, trials, wide), jnp.float32),
-            pltpu.VMEM((n - 1, trials, wide), jnp.float32),
+            pltpu.VMEM((VB, 2 * pair_dev, band, columns), jnp.bfloat16),
+            pltpu.VMEM((2 * pair_dev * band, full), jnp.float32),
+            pltpu.VMEM((2, pair_dev * band, n * full), jnp.bfloat16),
+            pltpu.VMEM((every, n * full), jnp.bfloat16),
+            pltpu.VMEM((every, n * full), jnp.bfloat16),
+            pltpu.VMEM((n, parts, trials, full), jnp.float32),
+            pltpu.VMEM((parts - 1, n, trials, full), jnp.float32),
+            pltpu.VMEM((n, trials, full), jnp.float32),
+            pltpu.VMEM((n - 1, trials, full), jnp.float32),
             dma((n, parts - 1)), dma((n, parts - 1)), dma((n - 1,)), dma((n - 1,)),
         ],
         compiler_params=pltpu.CompilerParams(collective_id=1, has_side_effects=True, vmem_limit_bytes=48 * 1024 * 1024),
     )(
-        position, jnp.take(kpoint_slot, kpairs[:, 0]), jnp.take(kpoint_slot, kpairs[:, 1]),
-        kernel.reshape(slot_count, rows, columns), x_all, mask, spread, put.astype(jnp.bfloat16),
+        position, jnp.take(kpoint_slot, kpairs[:, 1]), kernel.reshape(slot_count, rows, columns), x_all,
+        jnp.asarray(mask), jnp.asarray(spread), near.astype(jnp.bfloat16), pick.astype(jnp.bfloat16),
     )
     return result.reshape(1, trials * wide)
 

time: 143 us -> 139 us (0.972)
  Pallas kernels: 133 us -> 128 us
    pallas_call x1, Pallas kernels: 30.3 us -> 25 us  [ringed(): pl.pallas_call(functools.partial(response_kernel, n, parts), out_shape=ja...]
where the time goes in v3:
time: 139 us
  Pallas kernels  128 us (92%)
  other arithmetic  5.95 us (4%)
  local copies, waits for them, and re-layouts  5.11 us (4%)
    pallas_call x1, Pallas kernels, ringed(): pl.pallas_call(functools.partial(kernel_blocks_kernel, n, parts, capacity...  103 us
    pallas_call x1, Pallas kernels, ringed(): pl.pallas_call(functools.partial(response_kernel, n, parts), out_shape=ja...  25 us

profile of v3, /device:TPU:0, one launch (start us, length us, event | category | flops | bytes accessed | tf_op | source)
XLA Modules:
  0.0 138.8 jit_solution(1599849203365799295)
XLA Ops:
  0.0 0.0 copy-start
  0.0 0.8 compare_select_fusion
  0.8 0.0 copy-done
  0.8 0.7 gather_fusion
  1.5 0.7 gather_fusion.1
  2.2 0.8 and_select_fusion
  3.0 0.1 broadcast_in_dim.44
  3.0 0.1 eq.60
  3.1 1.2 select_convert_fusion.1.near_ref
  4.3 0.9 convert_reduce_fusion
  5.2 0.7 multiply_add_fusion.position_ref
  5.9 0.6 select_reduce_fusion.source_ref
  6.5 0.8 reduce
  7.2 0.7 reshape.27.x_ref
  7.9 0.0 copy-start.7
  7.9 0.0 copy-start.5
  7.9 0.0 copy-start.6
  7.9 0.0 copy-start.3
  7.9 0.0 copy-start.4
  7.9 102.6 %shard_map.136 = (f32[8,6,16,196]{3,2,1,0:T(8,128)}, f32[4,8,32,112]{3,2,1,0:T(8,128)}) custom-call(s32[48]{0:T(128)} %select_reduce_fusion.source_ref, f32[26,16,1024]{2,1,0:T(8,128)} %v_ref.1, bf16[26,196,256]{2,1,0:T(8,128)(2,1)} %c_ref.1, f32[1,1024,1024]{2,1,0:T(8,128)} %w_ref.1, f32[32,112]{1,0:T(8,128)} %reshape.27.x_ref), custom_call_target="tpu_custom_call" | custom-call | tf_op jit(solution)/shard_map/pallas_call | solution.py:323
  110.6 0.0 copy-done.7
  110.6 0.0 copy-done.5
  110.6 0.0 copy-done.6
  110.6 0.3 select_convert_fusion.pick_ref
  110.9 0.0 copy-done.3
  110.9 0.0 copy-done.4
  110.9 0.0 copy-start.1
  110.9 1.1 copy-done.1
  112.1 0.0 copy-start.2
  112.1 1.0 copy-done.2
  113.1 25.0 %shard_map.137 = f32[32,112]{1,0:T(8,128)S(1)} custom-call(s32[26]{0:T(128)S(1)} %multiply_add_fusion.position_ref, s32[26]{0:T(128)S(1)} %get-tuple-element.11.far_ref, f32[48,16,196]{2,1,0:T(8,128)S(1)} %bitcast.11, f32[4,8,32,112]{3,2,1,0:T(8,128)S(1)} %copy-done.2, f32[16,196]{1,0:T(8,128)S(1)} %copy-done.4, bf16[8,196,128]{2,1,0:T(8,128)(2,1)S(1)} %copy-done.3, ...), custom_call_target="tpu_custom_call" | custom-call | tf_op jit(solution)/shard_map/pallas_call | solution.py:370
  138.1 0.7 reshape.29
  (2 shorter events, 0.0 us)
Async XLA Ops:
  0.0 0.8 copy-start
  7.9 102.7 %copy-start.7 = (s32[256]{0:T(256)S(1)}, s32[256]{0:T(256)}, u32[]{:S(2)}) copy-start(s32[256]{0:T(256)} %constant.19.clone) | copy-start | bytes 3076
  7.9 102.7 %copy-start.5 = (pred[256,1024]{1,0:T(32,128)(4,1)S(1)}, pred[256,1024]{1,0:T(32,128)(4,1)}, u32[]{:S(2)}) copy-start(pred[256,1024]{1,0:T(32,128)(4,1)} %constant.18.clone) | copy-start | bytes 786436
  7.9 102.7 %copy-start.6 = (s32[1024]{0:T(1024)S(1)}, s32[1024]{0:T(1024)}, u32[]{:S(2)}) copy-start(s32[1024]{0:T(1024)} %constant.40.clone) | copy-start | bytes 12292
  7.9 103.0 %copy-start.3 = (bf16[8,196,128]{2,1,0:T(8,128)(2,1)S(1)}, bf16[8,196,128]{2,1,0:T(8,128)(2,1)}, u32[]{:S(2)}) copy-start(bf16[8,196,128]{2,1,0:T(8,128)(2,1)} %constant.44.clone.spread_ref) | copy-start | bytes 1204228
  7.9 103.0 %copy-start.4 = (f32[16,196]{1,0:T(8,128)S(1)}, f32[16,196]{1,0:T(8,128)}, u32[]{:S(2)}) copy-start(f32[16,196]{1,0:T(8,128)} %constant.43.clone.mask_ref) | copy-start | bytes 37636
  110.9 1.1 copy-start.1
  112.1 1.0 copy-start.2

commit v4 on v3

--- a/solution.py
+++ b/solution.py
@@ -31,23 +31,44 @@
     n, parts, capacity,
     source_ref, v_ref, c_ref, w_ref, x_ref,
     k_ref, xout_ref,
-    w_all, v_all, v_high, v_low, stacked, rows_of, k_part, k_in, x_all,
-    local_sems, v_send, v_recv, ring_send, ring_recv, k_send, k_recv, x_send, x_recv, xk_send, xk_recv,
+    w_main, w_cross, v_all, v_high, v_low, stacked, b_high, b_low, k_part, k_near, k_go, k_got, x_all,
+    local_sems, v_send, v_recv, ring_send, ring_recv, cross_send, cross_recv,
+    near_send, near_recv, go_send, go_recv, x_send, x_recv, xk_send, xk_recv,
 ):
     pb, ka = lax.axis_index("pb"), lax.axis_index("ka")
     place = jnp.where(pb % 2 == 0, pb // 2, n - 1 - pb // 2)
     right = ring_index((place + 1) % n, n)
     left = ring_index((place + n - 1) % n, n)
-    partner = ka + 1 - 2 * (ka % 2)
+    core = ka % 2
+    partner = ka + 1 - 2 * core
     across = (ka + 2) % parts
+    chip = ka - core
+    other = (chip + 2) % parts
     rows = v_ref.shape[1]
-    depth = w_all.shape[1]
+    depth = w_main.shape[1]
+    main = w_main.shape[2]
+    half = depth // 2
     pairs = v_ref.shape[0]
-
-    own_w = pltpu.make_async_copy(w_ref.at[0, pl.ds(pl.multiple_of(ka * depth, depth), depth), :], w_all.at[place], local_sems.at[0])
-    own_v = pltpu.make_async_copy(v_ref, v_all.at[ka], local_sems.at[1])
-    own_w.start()
-    own_v.start()
+    all_rows = parts * rows
+    span = capacity * all_rows
+
+    def at_block(index, count=1):
+        return pl.ds(pl.multiple_of(index * depth, depth), count * depth)
+
+    cross_rows = pl.ds(pl.multiple_of(core * half, half), half)
+    loads = [
+        pltpu.make_async_copy(w_ref.at[0, at_block(ka), at_block(ka)], w_main.at[place, :, pl.ds(0, depth)], local_sems.at[0]),
+        pltpu.make_async_copy(
+            w_ref.at[0, at_block(ka), at_block(other, 2)], w_main.at[place, :, pl.ds(depth, 2 * depth)], local_sems.at[1]
+        ),
+        pltpu.make_async_copy(
+            w_ref.at[0, pl.ds(pl.multiple_of(chip * depth + core * half, half), half), at_block(chip + 1)],
+            w_cross.at[place, cross_rows], local_sems.at[2],
+        ),
+        pltpu.make_async_copy(v_ref, v_all.at[ka], local_sems.at[3]),
+    ]
+    for load in loads:
+        load.start()
     x_all[ka, pb] = x_ref[...]
 
     barrier = pltpu.get_barrier_semaphore()
@@ -61,101 +82,111 @@
         return pltpu.make_async_remote_copy(src_ref=src, dst_ref=dst, send_sem=send, recv_sem=recv, device_id=to, device_id_type=MESH)
 
     def ring(step):
-        ahead = (place + n - step) % n
-        behind = (place + step) % n
-        if step < n // 2 - 1:
-            go, back = w_all.at[ahead], w_all.at[behind]
-        else:
-            go = w_all.at[ahead, pl.ds(0, depth // 2)]
-            back = w_all.at[behind, pl.ds(depth // 2, depth // 2)]
-        return (
-            remote(go, go, ring_send.at[step, 0], ring_recv.at[step, 0], (right, ka)),
-            remote(back, back, ring_send.at[step, 1], ring_recv.at[step, 1], (left, ka)),
-        )
-
-    own_v.wait()
+        found = []
+        for way, at, to in ((0, (place + n - step) % n, right), (1, (place + step) % n, left)):
+            if step < n // 2 - 1:
+                spans = (w_main.at[at], w_cross.at[at, cross_rows])
+            else:
+                quarter = half // 2
+                spans = (
+                    w_main.at[at, pl.ds(way * half, half)],
+                    w_cross.at[at, pl.ds(pl.multiple_of(core * half + way * quarter, quarter), quarter)],
+                )
+            found.append([
+                remote(part, part, ring_send.at[step, way, i], ring_recv.at[step, way, i], (to, ka)) for i, part in enumerate(spans)
+            ])
+        return found
+
+    def cross_copy(at):
+        part = w_cross.at[at, cross_rows]
+        return remote(part, part, cross_send.at[at], cross_recv.at[at], (pb, partner))
+
+    for load in loads:
+        load.wait()
     v_across = remote(v_all.at[ka], v_all.at[ka], v_send.at[1], v_recv.at[1], (pb, across))
     v_partner = remote(v_all.at[ka], v_all.at[ka], v_send.at[0], v_recv.at[0], (pb, partner))
     v_pass = remote(v_all.at[across], v_all.at[across], v_send.at[2], v_recv.at[2], (pb, partner))
-    own_w.wait()
     copies = ring(0)
-    copies[0].start()
-    copies[1].start()
+    for copy in copies[0] + copies[1]:
+        copy.start()
     v_across.start()
     v_partner.start()
+    cross_copy(place).start()
     x_copies = [
         remote(x_all.at[ka, pb], x_all.at[ka, pb], x_send.at[d - 1], x_recv.at[d - 1], ((pb + d) % n, ka)) for d in range(1, n)
     ]
     for copy in x_copies:
         copy.start()
 
-    two = 2 * rows
-    span = capacity * two
-    chip = ka - ka % 2
-    other = (chip + 2) % parts
-
-    def split(side):
-        base = chip if side == 0 else other
-
-        def one(p, carry):
-            for j in range(2):
-                high, low = halves(v_all[base + j, p])
-                v_high[side, p, pl.ds(j * rows, rows), :] = high
-                v_low[side, p, pl.ds(j * rows, rows), :] = low
-            return carry
-
-        lax.fori_loop(0, pairs, one, 0)
-
-    def k_copy(q, d):
-        if d == 0:
-            to, at = partner, (1 - ka % 2) * rows
-        elif d == 1:
-            to, at = across, two + (ka % 2) * rows
-        else:
-            to, at = (partner + 2) % parts, two + (1 - ka % 2) * rows
-        return remote(
-            k_part.at[q, :, pl.ds(pl.multiple_of(at, rows), rows), :], k_in.at[d, q], k_send.at[q, d], k_recv.at[q, d], (pb, to)
-        )
+    order = (ka, across, partner, (partner + 2) % parts)
+
+    def split(p, carry):
+        for i in range(parts):
+            pieces = ((at_block(ka), 0, depth), (at_block(other, 2), depth, 2 * depth), (at_block(partner), main, depth))
+            for columns, at, size in pieces:
+                high, low = halves(v_all[order[i], p, :, columns])
+                v_high[p, pl.ds(i * rows, rows), pl.ds(at, size)] = high
+                v_low[p, pl.ds(i * rows, rows), pl.ds(at, size)] = low
+        return carry
 
     def place_of(k):
         return (place + n + ((k + 1) // 2) * (2 * (k % 2) - 1)) % n
 
-    def screen(side, first, last):
-        def block(k, carry):
-            at = place_of(k)
-            q = ring_index(at, n)
-            high, low = halves(w_all[at])
-            for s in range(capacity):
-                p = source_ref[q * capacity + s]
-                stacked[pl.ds(s * two, two), :] = v_high[side, p]
-                stacked[pl.ds(span + s * two, two), :] = v_low[side, p]
-            both = dot_nt(stacked[...], high)
-            screened = both[:span] + (both[span:] + dot_nt(stacked[pl.ds(0, span), :], low))
-            s_high, s_low = halves(screened)
-            for s in range(capacity):
-                rows_of[at, s, pl.ds(side * two, two), :] = s_high[s * two:(s + 1) * two]
-                rows_of[at, s, pl.ds(2 * two + side * two, two), :] = s_low[s * two:(s + 1) * two]
-            if side == 1:
-                for s in range(capacity):
-                    both = dot_nt(rows_of[at, s], c_ref[source_ref[q * capacity + s]])
-                    k_part[q, s] = both[:2 * two] + both[2 * two:]
-                for d in range(parts - 1):
-                    k_copy(q, d).start()
+    def near_copy(q):
+        return remote(k_part.at[q, :, pl.ds(2 * rows, 2 * rows), :], k_near.at[q], near_send.at[q], near_recv.at[q], (pb, partner))
+
+    def go_copy(q):
+        return remote(k_go.at[q], k_got.at[q], go_send.at[q], go_recv.at[q], (pb, across))
+
+    def pass_on(k):
+        q = ring_index(place_of(k), n)
+        near_copy(q).wait()
+        for s in range(capacity):
+            k_go[q, s] = k_part[q, s, pl.ds(rows, rows), :] + k_near[q, s, pl.ds(rows, rows), :]
+        go_copy(q).start()
+
+    def block(k):
+        at = place_of(k)
+        q = ring_index(at, n)
+        for s in range(capacity):
+            p = source_ref[q * capacity + s]
+            stacked[pl.ds(s * all_rows, all_rows), :] = v_high[p]
+            stacked[pl.ds(span + s * all_rows, all_rows), :] = v_low[p]
+        high, low = halves(w_main[at])
+        b_high[:, pl.ds(0, main)] = high
+        b_low[:, pl.ds(0, main)] = low
+        cross_copy(at).wait()
+        between = w_cross[at]
+        high, low = halves(jnp.where(core == 0, between, between.T))
+        b_high[:, pl.ds(main, depth)] = high
+        b_low[:, pl.ds(main, depth)] = low
+        both = dot_nt(stacked[...], b_high[...])
+        screened = both[:span] + (both[span:] + dot_nt(stacked[pl.ds(0, span), :], b_low[...]))
+        s_high, s_low = halves(screened)
+        for s in range(capacity):
+            part = slice(s * all_rows, (s + 1) * all_rows)
+            conduct = c_ref[source_ref[q * capacity + s]]
+            k_part[q, s] = dot_nt(s_high[part], conduct) + dot_nt(s_low[part], conduct)
+        near_copy(q).start()
+
+    def blocks(first, last):
+        def one(k, carry):
+            block(k)
+            pass_on(k - 1)
             return carry
 
-        lax.fori_loop(first, last, block, 0)
-
-    v_partner.wait()
-    split(0)
-    screen(0, 0, 1)
+        lax.fori_loop(first, last, one, 0)
+
     for step in range(1, n // 2):
         later = ring(step)
-        copies[0].wait_recv()
-        later[0].start()
-        copies[1].wait_recv()
-        later[1].start()
-        copies[0].wait_send()
-        copies[1].wait_send()
+        for way in range(2):
+            for copy in copies[way]:
+                copy.wait_recv()
+            for copy in later[way]:
+                copy.start()
+            cross_copy(place_of(2 * step - way)).start()
+        for copy in copies[0] + copies[1]:
+            copy.wait_send()
         copies = later
         if step == 1:
             for copy in x_copies:
@@ -166,35 +197,29 @@
             ]
             for copy in xk_copies:
                 copy.start()
-        if step < n // 2 - 2:
-            screen(0, 2 * step - 1, 2 * step + 1)
-        if step == n // 2 - 3:
+        if step == n // 2 - 2:
             v_across.wait()
             v_pass.start()
-        if step == n // 2 - 2:
+            v_partner.wait()
             v_pass.wait()
-            split(1)
-            screen(1, 0, n - 5)
-            screen(0, n - 5, n - 3)
+            lax.fori_loop(0, pairs, split, 0)
+            block(0)
+            blocks(1, n - 4)
+        if step == n // 2 - 1:
+            blocks(n - 4, n - 1)
             for copy in xk_copies:
                 copy.wait()
             xout_ref[...] = x_all[...]
-        if step == n // 2 - 1:
-            screen(1, n - 5, n - 3)
-            screen(0, n - 3, n - 1)
-            screen(1, n - 3, n - 1)
-    copies[0].wait()
-    copies[1].wait()
-    screen(0, n - 1, n)
-    screen(1, n - 1, n)
-
-    mine = pl.ds(pl.multiple_of((ka % 2) * rows, rows), rows)
+    for copy in copies[0] + copies[1]:
+        copy.wait()
+    cross_copy(place_of(n - 1)).start()
+    blocks(n - 1, n)
+    pass_on(n - 1)
 
     def total(q, carry):
-        for d in range(parts - 1):
-            k_copy(q, d).wait()
+        go_copy(q).wait()
         for s in range(capacity):
-            k_ref[q, s] = k_part[q, s, mine, :] + (k_in[0, q, s] + (k_in[1, q, s] + k_in[2, q, s]))
+            k_ref[q, s] = (k_part[q, s, pl.ds(0, rows), :] + k_near[q, s, pl.ds(0, rows), :]) + k_got[q, s]
         return carry
 
     lax.fori_loop(0, n, total, 0)
@@ -329,17 +354,21 @@
         in_specs=[pl.BlockSpec(memory_space=pltpu.SMEM), any_space, vmem, any_space, vmem],
         out_specs=(vmem, vmem),
         scratch_shapes=[
-            pltpu.VMEM((n, depth, waves), jnp.float32),
+            pltpu.VMEM((n, depth, waves - depth), jnp.float32),
+            pltpu.VMEM((n, depth, depth), jnp.float32),
             pltpu.VMEM((parts, pair_dev, rows, waves), jnp.float32),
-            pltpu.VMEM((2, pair_dev, 2 * rows, waves), jnp.bfloat16),
-            pltpu.VMEM((2, pair_dev, 2 * rows, waves), jnp.bfloat16),
-            pltpu.VMEM((capacity * 4 * rows, waves), jnp.bfloat16),
-            pltpu.VMEM((n, capacity, 8 * rows, depth), jnp.bfloat16),
+            pltpu.VMEM((pair_dev, parts * rows, waves), jnp.bfloat16),
+            pltpu.VMEM((pair_dev, parts * rows, waves), jnp.bfloat16),
+            pltpu.VMEM((2 * capacity * parts * rows, waves), jnp.bfloat16),
+            pltpu.VMEM((depth, waves), jnp.bfloat16),
+            pltpu.VMEM((depth, waves), jnp.bfloat16),
             pltpu.VMEM((n, capacity, parts * rows, columns), jnp.float32),
-            pltpu.VMEM((parts - 1, n, capacity, rows, columns), jnp.float32),
+            pltpu.VMEM((n, capacity, 2 * rows, columns), jnp.float32),
+            pltpu.VMEM((n, capacity, rows, columns), jnp.float32),
+            pltpu.VMEM((n, capacity, rows, columns), jnp.float32),
             pltpu.VMEM((parts, n, trials, wide), jnp.float32),
-            dma((2,)), dma((3,)), dma((3,)), dma((n // 2, 2)), dma((n // 2, 2)),
-            dma((n, parts - 1)), dma((n, parts - 1)), dma((n - 1,)), dma((n - 1,)), dma((parts - 1,)), dma((parts - 1,)),
+            dma((4,)), dma((3,)), dma((3,)), dma((n // 2, 2, 2)), dma((n // 2, 2, 2)), dma((n,)), dma((n,)),
+            dma((n,)), dma((n,)), dma((n,)), dma((n,)), dma((n - 1,)), dma((n - 1,)), dma((parts - 1,)), dma((parts - 1,)),
         ],
         compiler_params=pltpu.CompilerParams(collective_id=0, has_side_effects=True, vmem_limit_bytes=56 * 1024 * 1024),
     )(source, valence, conduction, screened, trial_blocks.reshape(trials, wide))

time: 139 us -> 128 us (0.921)
  Pallas kernels: 128 us -> 116 us
    pallas_call x1, Pallas kernels: 103 us -> 92.9 us  [ringed(): pl.pallas_call(functools.partial(kernel_blocks_kernel, n, parts, capacity...]
    pallas_call x1, Pallas kernels: 25 us -> 23.4 us  [ringed(): pl.pallas_call(functools.partial(response_kernel, n, parts), out_shape=ja...]
where the time goes in v4:
time: 128 us; the launch traced here: 127 us
  Pallas kernels  116 us (91%)
  other arithmetic  5.95 us (5%)
  local copies, waits for them, and re-layouts  5.11 us (4%)
    pallas_call x1, Pallas kernels, ringed(): pl.pallas_call(functools.partial(kernel_blocks_kernel, n, parts, capacity...  92.9 us
    pallas_call x1, Pallas kernels, ringed(): pl.pallas_call(functools.partial(response_kernel, n, parts), out_shape=ja...  23.4 us

profile of v4, /device:TPU:0, one launch (start us, length us, event | category | flops | bytes accessed | tf_op | source)
XLA Modules:
  0.0 127.5 jit_solution(4967481113485579713)
XLA Ops:
  0.0 0.0 copy-start
  0.0 0.8 compare_select_fusion
  0.8 0.0 copy-done
  0.8 0.7 gather_fusion
  1.5 0.7 gather_fusion.1
  2.2 0.8 and_select_fusion
  3.0 0.1 broadcast_in_dim.44
  3.0 0.1 eq.60
  3.1 1.2 select_convert_fusion.1.near_ref
  4.3 0.9 convert_reduce_fusion
  5.2 0.7 multiply_add_fusion.position_ref
  5.9 0.6 select_reduce_fusion.source_ref
  6.5 0.8 reduce
  7.2 0.7 reshape.27.x_ref
  7.9 0.0 copy-start.7
  7.9 0.0 copy-start.5
  7.9 0.0 copy-start.6
  7.9 0.0 copy-start.3
  7.9 0.0 copy-start.4
  7.9 92.9 %shard_map.136 = (f32[8,6,16,196]{3,2,1,0:T(8,128)}, f32[4,8,32,112]{3,2,1,0:T(8,128)}) custom-call(s32[48]{0:T(128)} %select_reduce_fusion.source_ref, f32[26,16,1024]{2,1,0:T(8,128)} %v_ref.1, bf16[26,196,256]{2,1,0:T(8,128)(2,1)} %c_ref.1, f32[1,1024,1024]{2,1,0:T(8,128)} %w_ref.1, f32[32,112]{1,0:T(8,128)} %reshape.27.x_ref), custom_call_target="tpu_custom_call" | custom-call | tf_op jit(solution)/shard_map/pallas_call | solution.py:348
  100.8 0.0 copy-done.7
  100.8 0.0 copy-done.5
  100.8 0.0 copy-done.6
  100.8 0.3 select_convert_fusion.pick_ref
  101.1 0.0 copy-done.3
  101.1 0.0 copy-done.4
  101.2 0.0 copy-start.1
  101.2 1.1 copy-done.1
  102.3 0.0 copy-start.2
  102.3 1.0 copy-done.2
  103.3 23.4 %shard_map.137 = f32[32,112]{1,0:T(8,128)S(1)} custom-call(s32[26]{0:T(128)S(1)} %multiply_add_fusion.position_ref, s32[26]{0:T(128)S(1)} %get-tuple-element.11.far_ref, f32[48,16,196]{2,1,0:T(8,128)S(1)} %bitcast.11, f32[4,8,32,112]{3,2,1,0:T(8,128)S(1)} %copy-done.2, f32[16,196]{1,0:T(8,128)S(1)} %copy-done.4, bf16[8,196,128]{2,1,0:T(8,128)(2,1)S(1)} %copy-done.3, ...), custom_call_target="tpu_custom_call" | custom-call | tf_op jit(solution)/shard_map/pallas_call | solution.py:399
  126.8 0.7 reshape.29
  (2 shorter events, 0.0 us)
Async XLA Ops:
  0.0 0.8 copy-start
  7.9 92.9 %copy-start.7 = (s32[256]{0:T(256)S(1)}, s32[256]{0:T(256)}, u32[]{:S(2)}) copy-start(s32[256]{0:T(256)} %constant.19.clone) | copy-start | bytes 3076
  7.9 92.9 %copy-start.5 = (pred[256,1024]{1,0:T(32,128)(4,1)S(1)}, pred[256,1024]{1,0:T(32,128)(4,1)}, u32[]{:S(2)}) copy-start(pred[256,1024]{1,0:T(32,128)(4,1)} %constant.18.clone) | copy-start | bytes 786436
  7.9 92.9 %copy-start.6 = (s32[1024]{0:T(1024)S(1)}, s32[1024]{0:T(1024)}, u32[]{:S(2)}) copy-start(s32[1024]{0:T(1024)} %constant.40.clone) | copy-start | bytes 12292
  7.9 93.2 %copy-start.3 = (bf16[8,196,128]{2,1,0:T(8,128)(2,1)S(1)}, bf16[8,196,128]{2,1,0:T(8,128)(2,1)}, u32[]{:S(2)}) copy-start(bf16[8,196,128]{2,1,0:T(8,128)(2,1)} %constant.44.clone.spread_ref) | copy-start | bytes 1204228
  7.9 93.2 %copy-start.4 = (f32[16,196]{1,0:T(8,128)S(1)}, f32[16,196]{1,0:T(8,128)}, u32[]{:S(2)}) copy-start(f32[16,196]{1,0:T(8,128)} %constant.43.clone.mask_ref) | copy-start | bytes 37636
  101.2 1.1 copy-start.1
  102.3 1.0 copy-start.2

commit v5 on v4

--- a/solution.py
+++ b/solution.py
@@ -120,8 +120,8 @@
 
     order = (ka, across, partner, (partner + 2) % parts)
 
-    def split(p, carry):
-        for i in range(parts):
+    def split(kinds, p, carry):
+        for i in kinds:
             pieces = ((at_block(ka), 0, depth), (at_block(other, 2), depth, 2 * depth), (at_block(partner), main, depth))
             for columns, at, size in pieces:
                 high, low = halves(v_all[order[i], p, :, columns])
@@ -177,13 +177,14 @@
 
         lax.fori_loop(first, last, one, 0)
 
+    v_partner.wait()
+    lax.fori_loop(0, pairs, functools.partial(split, (0, 2)), 0)
     for step in range(1, n // 2):
         later = ring(step)
         for way in range(2):
-            for copy in copies[way]:
-                copy.wait_recv()
-            for copy in later[way]:
-                copy.start()
+            for landed, follow in zip(copies[way], later[way]):
+                landed.wait_recv()
+                follow.start()
             cross_copy(place_of(2 * step - way)).start()
         for copy in copies[0] + copies[1]:
             copy.wait_send()
@@ -200,16 +201,15 @@
         if step == n // 2 - 2:
             v_across.wait()
             v_pass.start()
-            v_partner.wait()
             v_pass.wait()
-            lax.fori_loop(0, pairs, split, 0)
+            lax.fori_loop(0, pairs, functools.partial(split, (1, 3)), 0)
             block(0)
-            blocks(1, n - 4)
-        if step == n // 2 - 1:
-            blocks(n - 4, n - 1)
+            blocks(1, n - 5)
             for copy in xk_copies:
                 copy.wait()
             xout_ref[...] = x_all[...]
+        if step == n // 2 - 1:
+            blocks(n - 5, n - 1)
     for copy in copies[0] + copies[1]:
         copy.wait()
     cross_copy(place_of(n - 1)).start()

time: 128 us -> 128 us (level)
  no operation moved by 1% of the time
where the time goes in v5:
time: 128 us
  Pallas kernels  116 us (91%)
  other arithmetic  5.95 us (5%)
  local copies, waits for them, and re-layouts  5.11 us (4%)
    pallas_call x1, Pallas kernels, ringed(): pl.pallas_call(functools.partial(kernel_blocks_kernel, n, parts, capacity...  92.8 us
    pallas_call x1, Pallas kernels, ringed(): pl.pallas_call(functools.partial(response_kernel, n, parts), out_shape=ja...  23.5 us

profile of v5, /device:TPU:0, one launch (start us, length us, event | category | flops | bytes accessed | tf_op | source)
XLA Modules:
  0.0 127.5 jit_solution(12263160186263278787)
XLA Ops:
  0.0 0.0 copy-start
  0.0 0.8 compare_select_fusion
  0.8 0.0 copy-done
  0.8 0.7 gather_fusion
  1.5 0.7 gather_fusion.1
  2.2 0.8 and_select_fusion
  3.0 0.1 broadcast_in_dim.44
  3.0 0.1 eq.60
  3.1 1.2 select_convert_fusion.1.near_ref
  4.3 0.9 convert_reduce_fusion
  5.2 0.7 multiply_add_fusion.position_ref
  5.9 0.6 select_reduce_fusion.source_ref
  6.5 0.8 reduce
  7.2 0.7 reshape.27.x_ref
  7.9 0.0 copy-start.7
  7.9 0.0 copy-start.5
  7.9 0.0 copy-start.6
  7.9 0.0 copy-start.3
  7.9 0.0 copy-start.4
  7.9 92.8 %shard_map.136 = (f32[8,6,16,196]{3,2,1,0:T(8,128)}, f32[4,8,32,112]{3,2,1,0:T(8,128)}) custom-call(s32[48]{0:T(128)} %select_reduce_fusion.source_ref, f32[26,16,1024]{2,1,0:T(8,128)} %v_ref.1, bf16[26,196,256]{2,1,0:T(8,128)(2,1)} %c_ref.1, f32[1,1024,1024]{2,1,0:T(8,128)} %w_ref.1, f32[32,112]{1,0:T(8,128)} %reshape.27.x_ref), custom_call_target="tpu_custom_call" | custom-call | tf_op jit(solution)/shard_map/pallas_call | solution.py:348
  100.8 0.0 copy-done.7
  100.8 0.0 copy-done.5
  100.8 0.0 copy-done.6
  100.8 0.3 select_convert_fusion.pick_ref
  101.1 0.0 copy-done.3
  101.1 0.0 copy-done.4
  101.1 0.0 copy-start.1
  101.1 1.1 copy-done.1
  102.3 0.0 copy-start.2
  102.3 1.0 copy-done.2
  103.3 23.5 %shard_map.137 = f32[32,112]{1,0:T(8,128)S(1)} custom-call(s32[26]{0:T(128)S(1)} %multiply_add_fusion.position_ref, s32[26]{0:T(128)S(1)} %get-tuple-element.11.far_ref, f32[48,16,196]{2,1,0:T(8,128)S(1)} %bitcast.11, f32[4,8,32,112]{3,2,1,0:T(8,128)S(1)} %copy-done.2, f32[16,196]{1,0:T(8,128)S(1)} %copy-done.4, bf16[8,196,128]{2,1,0:T(8,128)(2,1)S(1)} %copy-done.3, ...), custom_call_target="tpu_custom_call" | custom-call | tf_op jit(solution)/shard_map/pallas_call | solution.py:399
  126.8 0.7 reshape.29
  (2 shorter events, 0.0 us)
Async XLA Ops:
  0.0 0.8 copy-start
  7.9 92.9 %copy-start.7 = (s32[256]{0:T(256)S(1)}, s32[256]{0:T(256)}, u32[]{:S(2)}) copy-start(s32[256]{0:T(256)} %constant.19.clone) | copy-start | bytes 3076
  7.9 92.9 %copy-start.5 = (pred[256,1024]{1,0:T(32,128)(4,1)S(1)}, pred[256,1024]{1,0:T(32,128)(4,1)}, u32[]{:S(2)}) copy-start(pred[256,1024]{1,0:T(32,128)(4,1)} %constant.18.clone) | copy-start | bytes 786436
  7.9 92.9 %copy-start.6 = (s32[1024]{0:T(1024)S(1)}, s32[1024]{0:T(1024)}, u32[]{:S(2)}) copy-start(s32[1024]{0:T(1024)} %constant.40.clone) | copy-start | bytes 12292
  7.9 93.2 %copy-start.3 = (bf16[8,196,128]{2,1,0:T(8,128)(2,1)S(1)}, bf16[8,196,128]{2,1,0:T(8,128)(2,1)}, u32[]{:S(2)}) copy-start(bf16[8,196,128]{2,1,0:T(8,128)(2,1)} %constant.44.clone.spread_ref) | copy-start | bytes 1204228
  7.9 93.2 %copy-start.4 = (f32[16,196]{1,0:T(8,128)S(1)}, f32[16,196]{1,0:T(8,128)}, u32[]{:S(2)}) copy-start(f32[16,196]{1,0:T(8,128)} %constant.43.clone.mask_ref) | copy-start | bytes 37636
  101.1 1.1 copy-start.1
  102.3 1.0 copy-start.2

commit v6 on v5

--- a/solution.py
+++ b/solution.py
@@ -227,7 +227,7 @@
 
 def response_kernel(
     n, parts,
-    position_ref, far_ref, k_ref, x_ref, mask_ref, spread_ref, near_ref, pick_ref,
+    position_ref, kpairs_ref, slot_ref, k_ref, x_ref, mask_ref, spread_ref, near_ref, pick_ref,
     out_ref,
     wide_rows, mixed, by_far, x_high, x_low, given, landed, joined, landed_pb,
     ka_send, ka_recv, pb_send, pb_recv,
@@ -278,8 +278,9 @@
     def cut(p, carry):
         at = pl.multiple_of(p * band, band)
         value = mixed[pl.ds(at, band), :] + mixed[pl.ds(pl.multiple_of((pairs + p) * band, band), band), :]
+        far = slot_ref[kpairs_ref[p, 1]]
         for m in range(n):
-            high, low = halves(value * (far_ref[p] == m).astype(jnp.float32))
+            high, low = halves(value * (far == m).astype(jnp.float32))
             by_far[0, pl.ds(at, band), pl.ds(m * full, full)] = high
             by_far[1, pl.ds(at, band), pl.ds(m * full, full)] = low
         return carry
@@ -399,7 +400,7 @@
     result = pl.pallas_call(
         functools.partial(response_kernel, n, parts),
         out_shape=jax.ShapeDtypeStruct((trials, wide), jnp.float32),
-        in_specs=[smem] * 2 + [vmem] * 6,
+        in_specs=[smem] * 3 + [vmem] * 6,
         out_specs=vmem,
         scratch_shapes=[
             pltpu.VMEM((VB, 2 * pair_dev, band, columns), jnp.bfloat16),
@@ -415,7 +416,7 @@
         ],
         compiler_params=pltpu.CompilerParams(collective_id=1, has_side_effects=True, vmem_limit_bytes=48 * 1024 * 1024),
     )(
-        position, jnp.take(kpoint_slot, kpairs[:, 1]), kernel.reshape(slot_count, rows, columns), x_all,
+        position, kpairs, kpoint_slot, kernel.reshape(slot_count, rows, columns), x_all,
         jnp.asarray(mask), jnp.asarray(spread), near.astype(jnp.bfloat16), pick.astype(jnp.bfloat16),
     )
     return result.reshape(1, trials * wide)

time: 128 us -> 125 us (0.977)
  other arithmetic: 5.95 us -> 3.5 us
    select_n x2, other arithmetic: 1.53 us -> 0.01 us  [ringed(): slot_near = jnp.take(kpoint_slot, kpairs[:, 0])]
where the time goes in v6:
time: 125 us
  Pallas kernels  117 us (94%)
  local copies, waits for them, and re-layouts  4.53 us (4%)
  other arithmetic  3.5 us (3%)
    pallas_call x1, Pallas kernels, ringed(): pl.pallas_call(functools.partial(kernel_blocks_kernel, n, parts, capacity...  92.9 us
    pallas_call x1, Pallas kernels, ringed(): pl.pallas_call(functools.partial(response_kernel, n, parts), out_shape=ja...  23.9 us

profile of v6, /device:TPU:0, one launch (start us, length us, event | category | flops | bytes accessed | tf_op | source)
XLA Modules:
  0.0 125.0 jit_solution(18442660725651213458)
XLA Ops:
  0.0 0.9 convert_reduce_fusion
  0.9 0.7 multiply_add_fusion.position_ref
  1.6 0.6 select_reduce_fusion.source_ref
  2.2 0.8 reduce
  2.9 0.7 reshape.26.x_ref
  3.6 0.0 copy-start.10
  3.6 0.0 copy-start.7
  3.6 0.0 copy-start
  3.6 0.0 copy-start.6
  3.6 0.0 copy-start.8
  3.7 0.0 copy-start.3
  3.7 0.0 copy-start.4
  3.7 92.9 %shard_map.136 = (f32[8,6,16,196]{3,2,1,0:T(8,128)}, f32[4,8,32,112]{3,2,1,0:T(8,128)}) custom-call(s32[48]{0:T(128)} %select_reduce_fusion.source_ref, f32[26,16,1024]{2,1,0:T(8,128)} %v_ref.1, bf16[26,196,256]{2,1,0:T(8,128)(2,1)} %c_ref.1, f32[1,1024,1024]{2,1,0:T(8,128)} %w_ref.1, f32[32,112]{1,0:T(8,128)} %reshape.26.x_ref), custom_call_target="tpu_custom_call" | custom-call | tf_op jit(solution)/shard_map/pallas_call | solution.py:349
  96.6 0.0 copy-done.10
  96.6 0.0 copy-done.5
  96.6 0.0 copy-done.7
  96.7 0.3 select_convert_fusion.pick_ref
  96.9 0.0 copy-done.9
  97.0 0.0 copy-done
  97.0 0.7 gather_fusion
  97.7 0.1 broadcast_in_dim.43
  97.8 0.1 eq.60
  97.8 0.0 copy-done.6
  97.8 0.0 copy-done.8
  97.8 0.3 select_convert_fusion.1.near_ref
  98.1 0.1 copy.17.kpairs_ref
  98.2 0.0 copy-done.3
  98.2 0.0 copy-done.4
  98.2 1.1 copy-done.1
  99.4 1.0 copy-done.2
  100.4 23.9 %shard_map.137 = f32[32,112]{1,0:T(8,128)S(1)} custom-call(s32[26]{0:T(128)S(1)} %multiply_add_fusion.position_ref, s32[26,2]{1,0:T(8,128)S(1)} %copy.17.kpairs_ref, s32[8]{0:T(128)S(1)} %copy-done, f32[48,16,196]{2,1,0:T(8,128)S(1)} %bitcast.7, f32[4,8,32,112]{3,2,1,0:T(8,128)S(1)} %copy-done.2, f32[16,196]{1,0:T(8,128)S(1)} %copy-done.4, ...), custom_call_target="tpu_custom_call" | custom-call | tf_op jit(solution)/shard_map/pallas_call | solution.py:400
  124.3 0.7 reshape.28
  (8 shorter events, 0.0 us)
Async XLA Ops:
  3.6 93.0 %copy-start.10 = (s32[256]{0:T(256)S(1)}, s32[256]{0:T(256)}, u32[]{:S(2)}) copy-start(s32[256]{0:T(256)} %constant.44.clone) | copy-start | bytes 3076
  3.6 93.0 %copy-start.5 = (pred[256,1024]{1,0:T(32,128)(4,1)S(1)}, pred[256,1024]{1,0:T(32,128)(4,1)}, u32[]{:S(2)}) copy-start(pred[256,1024]{1,0:T(32,128)(4,1)} %constant.43.clone) | copy-start | bytes 786436
  3.6 93.0 %copy-start.7 = (s32[1024]{0:T(1024)S(1)}, s32[1024]{0:T(1024)}, u32[]{:S(2)}) copy-start(s32[1024]{0:T(1024)} %constant.45.clone) | copy-start | bytes 12292
  3.6 93.3 %copy-start.9 = (s32[26,2]{0,1:T(2,128)S(1)}, s32[26,2]{0,1:T(2,128)}, u32[]{:S(2)}) copy-start(s32[26,2]{0,1:T(2,128)} %param.18) | copy-start | bytes 628
  3.6 93.4 %copy-start = (s32[8]{0:T(128)S(1)}, s32[8]{0:T(128)}, u32[]{:S(2)}) copy-start(s32[8]{0:T(128)} %slot_ref.1) | copy-start | bytes 100
  3.6 94.2 %copy-start.6 = (pred[256,832]{1,0:T(32,128)(4,1)S(1)}, pred[256,832]{1,0:T(32,128)(4,1)}, u32[]{:S(2)}) copy-start(pred[256,832]{1,0:T(32,128)(4,1)} %constant.46.clone) | copy-start | bytes 638980
  3.6 94.2 %copy-start.8 = (s32[256]{0:T(256)S(1)}, s32[256]{0:T(256)}, u32[]{:S(2)}) copy-start(s32[256]{0:T(256)} %constant.47.clone) | copy-start | bytes 3076
  3.7 94.6 %copy-start.3 = (bf16[8,196,128]{2,1,0:T(8,128)(2,1)S(1)}, bf16[8,196,128]{2,1,0:T(8,128)(2,1)}, u32[]{:S(2)}) copy-start(bf16[8,196,128]{2,1,0:T(8,128)(2,1)} %constant.49.clone.spread_ref) | copy-start | bytes 1204228
  3.7 94.6 %copy-start.4 = (f32[16,196]{1,0:T(8,128)S(1)}, f32[16,196]{1,0:T(8,128)}, u32[]{:S(2)}) copy-start(f32[16,196]{1,0:T(8,128)} %constant.48.clone.mask_ref) | copy-start | bytes 37636
  98.2 1.1 copy-start.1
  99.4 1.0 copy-start.2
